TPU v7x, 128 devices: a whole 4x4x4 slice. The times are simulated.
128 devices in a mesh: img: 16 (over y_hi, z, core), head: 8 (over x, y_lo).
Axes of the slice: x: 4, y: 4 (y_hi: 2, y_lo: 2; y = y_hi * 2 + y_lo), z: 4, core: 2. Of those that a mesh axis runs over, the one named last changes fastest.
Arguments:
- hidden: bfloat16 [3, 32, 8192], P(None, None, ('img', 'head')), may hold values from -6 to 6
- vision: bfloat16 [16, 4, 1600, 8192], P('img', None, 'head'), may hold values from -6 to 6
- image_ids: int32 [32], replicated, may hold values from 0 to 15, as said below
- tile_counts: int32 [16], replicated, may hold values from 1 to 4
- q_weight: bfloat16 [8192, 8192], P(('img', 'head')), may hold values from -0.0625 to 0.0625
- q_gain: float32 [8192], replicated, may hold values from 0.5 to 50, as said below
- k_weight: bfloat16 [8192, 1024], P('img'), may hold values from -0.0625 to 0.0625
- v_weight: bfloat16 [8192, 1024], P('img'), may hold values from -0.0625 to 0.0625
- o_weight: bfloat16 [8192, 8192], P('head', 'img'), may hold values from -0.0625 to 0.0625
Outputs:
- layer_out: float32 [3, 32, 8192], P(None, 'head', 'img')
Inputs may be any that keep to these rules, and one draw needn't show every extreme that they name: `image_ids`: each image is named by exactly two requests. `q_gain`: positive.
All inputs are finite; a program needn't handle non-finite values.
Results may differ from a plain program's by a relative error of at most 0.009.
The roundings to bfloat16 on the way count: a program that leaves them out, or rounds other values in their place, can miss the bound.
Values may be sent and summed in bfloat16 or wider, within the bound.
No kernel may reach another device: no remote copies, remote signals or barrier semaphores. Data moves between devices by JAX's collectives and lax.ppermute only.
A program may use at most 128 MiB of HBM per device.

v0:
```python
import jax
import jax.numpy as jnp
from jax import lax
from jax.sharding import PartitionSpec as P

HEADS = 64
KVH = 8
HD = 128
TILES = 4
STEPS = 3


EPS = 1e-05


def combined_all(value, axis, join):
    pieces = jax.tree.map(lambda part: lax.all_gather(part, axis), value)
    head = jax.tree.map(lambda part: part[0], pieces)
    tail = jax.tree.map(lambda part: part[1:], pieces)
    subtotal, _ = lax.scan(lambda subtotal, slab: (join(subtotal, slab), None), head, tail)
    return subtotal


def normalize(vectors):
    return vectors * lax.rsqrt(jnp.mean(vectors * vectors, axis=-1, keepdims=True) + EPS)


def softmax_join(first, second):
    max_first, total_first, sum_first = first
    max_second, total_second, sum_second = second
    peak = jnp.maximum(max_first, max_second)
    factor_first = jnp.exp(max_first - peak)
    factor_second = jnp.exp(max_second - peak)
    totals = total_first * factor_first + total_second * factor_second
    sums = sum_first * factor_first[..., None] + sum_second * factor_second[..., None]
    return (peak, totals, sums)


def per_device(
    hidden, vision, image_ids, tile_counts, q_weight, q_gain, k_weight, v_weight, o_weight
):
    img_pos = lax.axis_index("img")
    head_pos = lax.axis_index("head")
    per_group = HEADS // KVH
    requests = hidden.shape[1]
    img_dev = vision.shape[0]
    owned = 2 * img_dev
    tok_dev = vision.shape[2]
    block_width = o_weight.shape[0]
    order = jnp.arange(requests, dtype=jnp.int32)
    same_image = image_ids[:, None] == image_ids[None, :]
    earlier = order[None, :] < order[:, None]
    occurrence = jnp.sum(jnp.logical_and(same_image, earlier), axis=1)
    slot_of = 2 * image_ids + occurrence
    request_at = jnp.sum(jnp.where(slot_of[None, :] == order[:, None], order[None, :], 0), axis=1)
    partial_value = jnp.einsum("srd,de->sre", hidden, q_weight, preferred_element_type=jnp.float32)
    all_query = lax.psum(partial_value, ("img", "head"))
    own_rows = lax.dynamic_slice_in_dim(request_at, img_pos * owned, owned)
    own_query = jnp.take(all_query, own_rows, axis=1)
    own_query = own_query.reshape(STEPS, owned, HEADS, HD)
    queries = (normalize(own_query) * q_gain.reshape(HEADS, HD) * HD ** (-0.5)).astype(jnp.bfloat16)
    queries = queries.reshape(STEPS, img_dev, 2, KVH, per_group, HD)
    features = vision.reshape(img_dev * TILES * tok_dev, vision.shape[3])
    key_part = jnp.dot(
        features,
        lax.all_gather(k_weight, "img", axis=0, tiled=True),
        preferred_element_type=jnp.float32,
    )
    value_part = jnp.dot(
        features,
        lax.all_gather(v_weight, "img", axis=0, tiled=True),
        preferred_element_type=jnp.float32,
    )
    key_heads = normalize(key_part.reshape(img_dev, TILES * tok_dev, KVH, HD)).astype(jnp.bfloat16)
    value_heads = value_part.astype(jnp.bfloat16).reshape(img_dev, TILES * tok_dev, KVH, HD)
    local_limits = lax.dynamic_slice_in_dim(tile_counts, img_pos * img_dev, img_dev)
    tile_of = jnp.repeat(jnp.arange(TILES, dtype=jnp.int32), tok_dev)
    usable = tile_of[None, :] < local_limits[:, None]
    scores = jnp.einsum(
        "sgokhd,gtkd->sgokht", queries, key_heads, preferred_element_type=jnp.float32
    )
    scores = jnp.where(usable[None, :, None, None, None, :], scores, -jnp.inf)
    local_max = jnp.max(scores, axis=-1)
    expo = jnp.exp(scores - local_max[..., None])
    totals = jnp.sum(expo, axis=-1)
    weighted = jnp.einsum(
        "sgokht,gtkd->sgokhd",
        expo.astype(jnp.bfloat16),
        value_heads,
        preferred_element_type=jnp.float32,
    )
    peak, totals, weighted = combined_all((local_max, totals, weighted), "head", softmax_join)
    result = weighted / totals[..., None]
    result = result.reshape(STEPS, owned, HEADS * HD)
    result = lax.dynamic_slice_in_dim(result, head_pos * block_width, block_width, 2)
    attention = result.astype(jnp.bfloat16)
    terms = jnp.einsum(
        "srw,wd->srd",
        lax.all_gather(attention, "img", axis=1, tiled=True),
        o_weight,
        preferred_element_type=jnp.float32,
    )
    terms = jnp.take(terms, slot_of, axis=1)
    layer_out = lax.psum_scatter(terms, "head", scatter_dimension=1, tiled=True)
    return layer_out


def solution(mesh):
    placed = (
        P(None, None, ("img", "head")),
        P("img", None, "head", None),
        P(),
        P(),
        P(("img", "head"), None),
        P(),
        P("img", None),
        P("img", None),
        P("head", "img"),
    )
    return jax.shard_map(
        per_device, mesh=mesh, in_specs=placed, out_specs=P(None, "head", "img"), check_vma=False
    )
```

profile of v0, /device:TPU:0, one launch (start us, length us, event | category | flops | bytes accessed | tf_op | source)
XLA Modules:
  0.0 522.8 jit_solution(16519401923681423272)
XLA Ops:
  7.4 1.2 copy-done
  8.6 2.9 fusion.25
  11.6 0.5 all-gather.7.cloned.1.call-update
  12.2 0.5 all-gather.9.cloned.1.call-update
  12.8 0.6 dynamic_slice.20
  13.4 0.7 iota_compare_fusion.2
  14.0 0.7 lt.69
  14.9 0.6 compare_and_fusion.1
  16.1 278.5 %all-reduce.4.cloned.1.call-done = f32[3,32,8192]{2,1,0:T(8,128)} async-done(((f32[3,32,8192]{2,1,0:T(8,128)}), f32[3,32,8192]{2,1,0:T(8,128)}) %all-reduce.4.cloned.1.call-update) | async-done | bytes 3145744 | tf_op jit(solution)/shard_map/psum | solution.py:57
  294.5 6.1 %copy.96 = f32[3,32,8192]{2,0,1:T(4,128)} copy(f32[3,32,8192]{2,1,0:T(8,128)} %all-reduce.4.cloned.1.call-done) | data formatting | bytes 6291456 | tf_op jit(solution)/shard_map/psum | solution.py:57
  300.6 2.9 gather_fusion
  304.1 0.7 rsqrt.21
  304.8 18.5 %fusion.42 = f32[800,1024]{1,0:T(8,128)S(1)} fusion(bf16[800,8192]{1,0:T(8,128)(2,1)} %bitcast.134, bf16[8192,1024]{1,0:T(8,128)(2,1)} %all-gather.7.cloned.1.call-done), kind=kOutput, calls=%fused_computation.71 | convolution fusion | flops 13421772800 | bytes 33161216 | tf_op jit(solution)/shard_map/dot_general | solution.py:64
  323.7 2.5 copy.121
  326.2 3.6 reduce_sum.46
  329.8 1.1 copy.94
  331.0 18.8 %fusion.13 = bf16[100,8,8,128]{3,1,2,0:T(8,128)(2,1)S(1)} fusion(bf16[800,8192]{1,0:T(8,128)(2,1)} %bitcast.135, bf16[8192,1024]{1,0:T(8,128)(2,1)} %all-gather.9.cloned.1.call-done), kind=kOutput, calls=%fused_computation.23 | convolution fusion | flops 13422592000 | bytes 31522816 | tf_op jit(solution)/shard_map/dot_general | solution.py:69
  350.6 2.3 bitcast_reduce_fusion
  352.9 2.8 fusion.18
  355.8 1.7 fusion.22
  357.5 28.5 %all-gather = f32[24,2,8,8]{3,2,1,0:T(8,128)S(1)} all-gather(f32[3,2,8,8]{3,2,1,0:T(8,128)S(1)} %copy.100), channel_id=2, replica_groups=mesh['img'=16,'head'=8] {'head'}, dimensions={0}, use_global_device_ids=true | all-gather | bytes 13824 | tf_op jit(solution)/shard_map/all_gather | solution.py:17
  386.1 28.4 %all-gather.1 = f32[24,2,8,8]{3,2,1,0:T(8,128)S(1)} all-gather(f32[3,2,8,8]{3,2,1,0:T(8,128)S(1)} %copy.101), channel_id=3, replica_groups=mesh['img'=16,'head'=8] {'head'}, dimensions={0}, use_global_device_ids=true | all-gather | bytes 13824 | tf_op jit(solution)/shard_map/all_gather | solution.py:17
  414.6 1.1 slice.36
  416.0 2.1 while.14
  418.3 23.6 %all_gather.35 = bf16[3,32,1024]{2,0,1:T(4,128)(2,1)S(1)} all-gather(bf16[3,2,1024]{2,0,1:T(4,128)(2,1)S(1)} %copy.109), channel_id=1, replica_groups=mesh['img'=16,'head'=8] {'img'}, dimensions={1}, use_global_device_ids=true | all-gather | bytes 208896 | tf_op jit(solution)/shard_map/all_gather | solution.py:99
  441.9 1.5 fusion.23
  443.5 0.7 gather_fusion.1
  444.3 0.8 select_bitcast_fusion
  445.1 0.6 dynamic-slice
  446.4 67.9 %all-reduce.6.cloned.1.call-done = f32[3,32,512]{2,0,1:T(4,128)} async-done(((f32[3,32,512]{2,0,1:T(4,128)}), f32[3,32,512]{2,0,1:T(4,128)}) %all-reduce.6.cloned.1.call-update) | async-done | bytes 196624
  514.3 0.8 constant_dynamic-slice_fusion.1
  515.0 0.6 copy.112
  (91 shorter events, 5.3 us)
Async XLA Ops:
  7.4 1.2 copy-start
  7.4 287.2 %all-reduce.4.cloned.1.call-start = ((), (), s32[]{:S(2)}) async-start(), calls=%async_computation.1 | async-start | bytes 6291456 | tf_op jit(solution)/shard_map/psum | solution.py:57
  11.5 1.3 copy-start.11
  11.5 3.2 copy-start.8
  11.6 293.2 %all-gather.7.cloned.1.call-start = ((), (), s32[]{:S(2)}) async-start(), calls=%async_computation | async-start | bytes 17825792 | tf_op jit(solution)/shard_map/all_gather | solution.py:66
  12.1 318.9 %all-gather.9.cloned.1.call-start = ((), (), s32[]{:S(2)}) async-start(), calls=%async_computation.2 | async-start | bytes 17825792 | tf_op jit(solution)/shard_map/all_gather | solution.py:71
  12.7 401.8 %all-gather.11.cloned.1.call-start = ((), (), s32[]{:S(2)}) async-start(), calls=%async_computation.3 | async-start | bytes 1769472 | tf_op jit(solution)/shard_map/all_gather | solution.py:17
  15.5 0.6 copy-start.9
  16.0 287.8 %copy-start.5 = (pred[2]{0:T(512)(128)(4,1)}, pred[2]{0:T(512)(128)(4,1)S(1)}, u32[]{:S(2)}) copy-start(pred[2]{0:T(512)(128)(4,1)S(1)} %get-tuple-element.112) | copy-start | bytes 10
  349.8 0.7 copy-start.2
  349.8 0.8 copy-start.3
  349.8 0.8 copy-start.4
  349.8 0.7 copy-start.6
  352.9 2.8 copy-start.10
  355.7 158.6 %all-reduce.6.cloned.1.call-start = ((), (), s32[]{:S(2)}) async-start(), calls=%async_computation.4 | async-start | bytes 524288
  414.5 1.4 slice-start
  416.0 28.3 %copy-start.7 = (pred[32]{0:T(512)(128)(4,1)S(1)}, pred[32]{0:T(512)(128)(4,1)}, u32[]{:S(2)}) copy-start(pred[32]{0:T(512)(128)(4,1)} %get-tuple-element.110) | copy-start | bytes 100
  418.1 27.1 %copy-start.12 = (u32[128]{0:T(128)S(1)}, u32[128]{0:T(128)}, u32[]{:S(2)}) copy-start(u32[128]{0:T(128)} %constant.77) | copy-start | bytes 1540
  418.1 97.6 %copy-start.1 = (bf16[64,8192]{1,0:T(8,128)(2,1)S(1)}, bf16[64,8192]{1,0:T(8,128)(2,1)}, u32[]{:S(2)}) copy-start(bf16[64,8192]{1,0:T(8,128)(2,1)} %param.15) | copy-start | bytes 3145732
Sparse Core Ops, SparseCore 0:
  12.9 281.5 all-reduce.3
  355.8 45.2 all-gather.10
  445.2 68.9 all-reduce.5
Sparse Core Ops, SparseCore 1:
  14.8 112.6 all-gather.6
  130.1 106.7 all-gather.8
where the time goes:
time: 523 us
  waiting for transfers between devices  348 us (67%)
  blocking collectives  80.5 us (15%)
  matrix products  46.8 us (9%)
  local copies, waits for them, and re-layouts  21.6 us (4%)
  between operations  15.6 us (3%)
  other arithmetic  10.4 us (2%)
    psum x1, waiting for transfers between devices, per_device(): all_query = lax.psum(partial_value, ('img', 'head'))  278 us
    unnamed x6, waiting for transfers between devices  69 us
    all_gather x2, blocking collectives, combined_all(): pieces = jax.tree.map(lambda part: lax.all_gather(part, axis), value)  56.9 us
    all_gather x1, blocking collectives, per_device(): lax.all_gather(attention, 'img', axis=1, tiled=True)  23.6 us
    dot_general x1, matrix products, per_device(): jnp.dot(features, lax.all_gather(v_weight, 'img', axis=0, tiled=True), pr...  18.8 us
    dot_general x1, matrix products, per_device(): jnp.dot(features, lax.all_gather(k_weight, 'img', axis=0, tiled=True), pr...  18.5 us
  transfers between devices with their start and end apart: 5, of which 2 were waited for; matrix products, arithmetic and copies ran while one was open for 8% of the time, Pallas kernels for 0%

commit v1 on v0

v1 whole, which is shorter than its diff:
```python
import jax
import jax.numpy as jnp
from jax import lax
from jax.experimental import pallas as pl
from jax.experimental.pallas import tpu as pltpu
from jax.sharding import Mesh, PartitionSpec as P

HEADS = 64
KVH = 8
HD = 128
TILES = 4
STEPS = 3
EPS = 1e-05

AXES = ("yh", "z", "c", "x", "yl")
SIZES = (2, 4, 2, 4, 2)
F32 = jnp.float32
BF16 = jnp.bfloat16


def pair_a(v):
    return v ^ 1


def pair_b(v):
    return (((v + 1) ^ 1) - 1) % 4


def first(c, v):
    return pair_a(v) if c == 0 else pair_b(v)


def second(c, v):
    return pair_b(v) if c == 0 else pair_a(v)


def place(y, z, c, x):
    return ((((y // 2) * 4 + z) * 2 + c) * 4 + x) * 2 + (y % 2)


def table(move):
    return [
        (place(y, z, c, x), place(*move(y, z, c, x)))
        for y in range(4)
        for z in range(4)
        for c in range(2)
        for x in range(4)
    ]


CORE = table(lambda y, z, c, x: (y, z, 1 - c, x))
YC = table(lambda y, z, c, x: (pair_b(y), z, c, x))
YR = table(lambda y, z, c, x: (pair_a(y), z, c, x))
Z1 = table(lambda y, z, c, x: (y, first(c, z), c, x))
Z2 = table(lambda y, z, c, x: (y, second(c, z), c, x))
Y1 = table(lambda y, z, c, x: (first(c, y), z, c, x))
Y2 = table(lambda y, z, c, x: (second(c, y), z, c, x))
X1 = table(lambda y, z, c, x: (y, z, c, first(c, x)))
X2 = table(lambda y, z, c, x: (y, z, c, second(c, x)))


def send(value, moves):
    return lax.ppermute(value, AXES, moves)


def cat(*parts):
    return jnp.concatenate(parts, axis=0)


def mate(core, v, step):
    a = v ^ 1
    b = (((v + 1) ^ 1) + 3) % 4
    return jnp.where(core == step, a, b)


def take_rows(value, start, size):
    return lax.dynamic_slice_in_dim(value, start, size, 0)


def project(features, segments, index, size, total=None, norm=False, last=True):
    terms = len(segments[0][1])
    steps = sum(n for n, _ in segments)
    width = segments[0][1][0][0].shape[1]
    tokens = features[0].shape[0]
    arrays, in_specs, spans = [], [], []
    for t in range(terms):
        for value in features:
            arrays.append(value)
            in_specs.append(
                pl.BlockSpec((tokens, size), lambda i, idx, t=t: (0, idx[i * terms + t]))
            )
    start = 0
    for n, parts in segments:
        for value, offset, stride in parts:
            arrays.append(value)
            in_specs.append(
                pl.BlockSpec(
                    (size, width),
                    lambda i, idx, s=start, n=n, o=offset, m=stride: (
                        jnp.clip(i - s, 0, n - 1) * m + o,
                        0,
                    ),
                )
            )
        spans.append((start, start + n))
        start += n
    if total is not None:
        arrays.append(total)
        in_specs.append(pl.BlockSpec((2, tokens, width), lambda i, idx: (0, 0, 0)))

    def body(idx_ref, *refs):
        step = pl.program_id(0)
        left = refs[: 2 * terms]
        right = refs[2 * terms : 2 * terms + terms * len(segments)]
        out_ref, acc_ref = refs[-2:]

        @pl.when(step == 0)
        def _():
            if total is None:
                acc_ref[...] = jnp.zeros_like(acc_ref)
            else:
                acc_ref[...] = refs[-3][...]

        for k, (lo, hi) in enumerate(spans):

            @pl.when(jnp.logical_and(step >= lo, step < hi))
            def _(k=k):
                rows = [r[...] for r in right[k * terms : (k + 1) * terms]]
                rows = rows[0] if terms == 1 else jnp.concatenate(rows, axis=0)
                for i in range(2):
                    cols = [left[2 * t + i][...] for t in range(terms)]
                    cols = cols[0] if terms == 1 else jnp.concatenate(cols, axis=1)
                    acc_ref[i] += jnp.dot(cols, rows, preferred_element_type=F32)

        @pl.when(step == steps - 1)
        def _():
            if not last:
                out_ref[...] = acc_ref[...]
                return
            for i in range(2):
                for h in range(width // HD):
                    part = acc_ref[i, :, h * HD : (h + 1) * HD]
                    if norm:
                        mean = jnp.mean(part * part, axis=-1, keepdims=True)
                        part = part * lax.rsqrt(mean + EPS)
                    out_ref[i, :, h * HD : (h + 1) * HD] = part.astype(BF16)

    return pl.pallas_call(
        body,
        grid_spec=pltpu.PrefetchScalarGridSpec(
            num_scalar_prefetch=1,
            grid=(steps,),
            in_specs=in_specs,
            out_specs=pl.BlockSpec((2, tokens, width), lambda i, idx: (0, 0, 0)),
            scratch_shapes=[pltpu.VMEM((2, tokens, width), F32)],
        ),
        out_shape=jax.ShapeDtypeStruct((2, tokens, width), BF16 if last else F32),
        cost_estimate=pl.CostEstimate(
            flops=4 * tokens * size * terms * steps * width,
            bytes_accessed=4 * tokens * size * terms * steps,
            transcendentals=0,
        ),
        compiler_params=pltpu.CompilerParams(vmem_limit_bytes=52 * 1024 * 1024),
    )(jnp.stack(index).astype(jnp.int32), *arrays)


def project_keys(features, lower, upper, steps):
    tokens = features[0].shape[0]
    size, width = 512, 256
    count = len(steps)
    table = jnp.stack([jnp.stack([jnp.asarray(n, jnp.int32) for n in s]) for s in steps])
    span = count // 4

    def rows_at(column, busy):
        def at(i, idx):
            now = jnp.int32(0)
            for g in range(4):
                near = i - g * span
                use = jnp.clip(i, g * span, (g + 1) * span - 1)
                if g in busy:
                    now = jnp.where(
                        jnp.logical_or(near >= 0, g == min(busy)), idx[use * 3 + column], now
                    )
            return (now, 0)

        return at

    def body(idx_ref, m_ref, t_ref, l0, l1, u0, u1, out_ref, acc_ref):
        step = pl.program_id(0)

        @pl.when(step == 0)
        def _():
            acc_ref[...] = jnp.zeros_like(acc_ref)

        for g, (low, up) in enumerate(((l0, u0), (l0, u1), (l1, u0), (l1, u1))):

            @pl.when(step // span == g)
            def _(low=low, up=up):
                rows = jnp.concatenate([low[...], up[...]], axis=1)
                acc_ref[0] += jnp.dot(m_ref[...], rows, preferred_element_type=F32)
                acc_ref[1] += jnp.dot(t_ref[...], rows, preferred_element_type=F32)

        @pl.when(step == count - 1)
        def _():
            for i in range(2):
                for h in range(4):
                    part = acc_ref[i, :, h * HD : (h + 1) * HD]
                    mean = jnp.mean(part * part, axis=-1, keepdims=True)
                    out_ref[i, :, h * HD : (h + 1) * HD] = (part * lax.rsqrt(mean + EPS)).astype(BF16)

    column = pl.BlockSpec((tokens, size), lambda i, idx: (0, idx[i * 3]))
    shape = (2, tokens, 2 * width)
    return pl.pallas_call(
        body,
        grid_spec=pltpu.PrefetchScalarGridSpec(
            num_scalar_prefetch=1,
            grid=(count,),
            in_specs=[
                column,
                column,
                pl.BlockSpec((size, width), rows_at(1, (0, 1))),
                pl.BlockSpec((size, width), rows_at(1, (2, 3))),
                pl.BlockSpec((size, width), rows_at(2, (0, 2))),
                pl.BlockSpec((size, width), rows_at(2, (1, 3))),
            ],
            out_specs=pl.BlockSpec(shape, lambda i, idx: (0, 0, 0)),
            scratch_shapes=[pltpu.VMEM(shape, F32)],
        ),
        out_shape=jax.ShapeDtypeStruct(shape, BF16),
        cost_estimate=pl.CostEstimate(
            flops=8 * tokens * size * count * width,
            bytes_accessed=4 * tokens * size * count,
            transcendentals=0,
        ),
        compiler_params=pltpu.CompilerParams(vmem_limit_bytes=52 * 1024 * 1024),
    )(table.reshape(-1), *features, *lower, *upper)


def slots(core, v):
    one, two = mate(core, v, 0), mate(core, v, 1)
    return (v, one, two, mate(core, two, 0))


def after(value, *others):
    return lax.optimization_barrier((value,) + others)[0]


def per_device(
    hidden, vision, image_ids, tile_counts, q_weight, q_gain, k_weight, v_weight, o_weight
):
    pos = tuple(lax.axis_index(a) for a in AXES)
    yh, z, core, x, yl = pos
    zs, xs = slots(core, z), slots(core, x)
    ys = slots(core, yh * 2 + yl)
    requests = hidden.shape[1]
    order = jnp.arange(requests, dtype=jnp.int32)
    same_image = image_ids[:, None] == image_ids[None, :]
    earlier = order[None, :] < order[:, None]
    occurrence = jnp.sum(jnp.logical_and(same_image, earlier), axis=1)
    slot_of = 2 * image_ids + occurrence
    request_at = jnp.sum(jnp.where(slot_of[None, :] == order[:, None], order[None, :], 0), axis=1)

    def column_half(w, which, width):
        return lax.dynamic_slice_in_dim(w, which * width, width, 1)

    def leaving(one, two):
        zpairs = ((z, two), (one, zs[3]))
        places = [
            (h * 4 + zz) * 4 + k for zp in zpairs for h in (yh, 1 - yh) for zz in zp for k in range(4)
        ]
        rows = jnp.take(hidden, jnp.take(request_at, jnp.stack(places)), axis=1)
        return rows.transpose(1, 0, 2).reshape(96, 64)

    give = cat(column_half(k_weight, 1 - core, 512), column_half(v_weight, 1 - core, 512))
    got = send(give, CORE)
    others = leaving(zs[2], zs[1])
    q_give = jnp.dot(
        after(others, give), column_half(q_weight, 1 - core, 4096), preferred_element_type=F32
    )
    q_got = send(q_give, CORE)
    q_mine = jnp.dot(
        leaving(zs[1], zs[2]), column_half(q_weight, core, 4096), preferred_element_type=F32
    )
    mine = vision.reshape(800, 8192)
    got = after(got, q_give)
    k_mine, v_mine = column_half(k_weight, core, 512), column_half(v_weight, core, 512)
    k_theirs, v_theirs = got[:512], got[512:]
    a0 = jnp.where(core == yl, k_mine[:, :256], k_theirs[:, :256])
    b0 = cat(k_mine[:, 256:], k_theirs[:, 256:])
    c0 = jnp.where(core == x // 2, v_mine, v_theirs)
    c0 = take_rows(c0, (x % 2) * 256, 256)
    c1 = send(c0, YC)
    a1 = send(a0, Z1)
    b1 = send(after(b0, a0, c0), YC)
    theirs = send(after(mine, b0), CORE)
    a01 = cat(a0, after(a1, b0))
    a2 = send(a01, Z2)
    c01 = cat(c0, after(c1, a01))
    c2 = send(c01, Z1)
    a0123 = cat(a01, after(a2, c01))
    a4 = send(a0123, Y1)
    c12 = cat(c1, after(c2, a0123))
    d1 = send(c12, X1)
    c0123 = cat(c01, after(c2, c12))
    c3 = send(c0123, Z2)
    q1 = send(after(q_mine[48:], c0123) + q_got[48:], Z1)
    d12 = cat(c12, after(d1, c0123, theirs))
    d2 = send(d12, X2)
    b01 = cat(b0, after(b1, d12))
    b2 = send(b01, Z1)
    c3 = after(c3, b01)
    e1 = send(c3, X1)
    q2 = q_mine[:48] + q_got[:48] + after(q1, c3)
    q3 = send(q2[24:], YC)
    a01234 = cat(a0123, after(a4, q2))
    a5 = send(a01234, Y2)
    q4 = q2[:24] + after(q3, a01234)
    q5 = send(q4[12:], Z2)
    b0123 = cat(b01, after(b2, q4))
    b3 = send(b0123, Z2)
    q6 = q4[:12] + after(q5, b0123)
    q7 = send(q6, YR)
    features = (mine, theirs)

    def color(h, zz):
        return h * 4 + zz

    def both(zz):
        return [color(yh, zz), color(1 - yh, zz)]

    def quarters(places):
        return [p * 4 + xx for p in places for xx in xs]

    def shared(n, own, one, two):
        return (n, ((own, 0, 1), (one, 0, 1), (two, 0, 1), (two, n, 1)))

    halved = [(v_mine, 0, 1), (v_mine, 1, 1), (v_theirs, 0, 1), (v_theirs, 1, 1)]
    index = [(color(yh, z) * 2 + cc) * 2 + t for cc in (core, 1 - core) for t in range(2)]
    index += quarters([color(1 - yh, z)] + both(zs[1]))
    values = project(
        features,
        [(1, tuple(halved)), shared(3, c12, d1, after(d2, q6))],
        index,
        256,
        last=False,
    )
    q8 = q6 + after(q7, values)
    q9 = send(q8, X1)
    e12 = cat(c3, after(e1, q8))
    e2 = send(e12, X2)
    steps = []
    for ks in ((0, 1), (2, 3)):
        for js in ((0, 1), (2, 3)):
            for k in ks:
                for j in js:
                    h, cc = ys[k] // 2, ys[k] % 2
                    spot = (j % 2) * 4 + jnp.where(h == yh, 0, 2) + jnp.where(cc == core, 0, 1)
                    steps.append((color(h, zs[j]) * 2 + cc, (k % 2) * 4 + j, spot))
    keys = project_keys(features, (a01234, after(a5, e12)), (b0123, b3), steps)
    q10 = q8 + after(q9, keys)
    q11 = send(q10, X2)
    value_heads = project(
        features,
        [shared(4, c3, e1, e2)],
        quarters(both(zs[2]) + both(zs[3])),
        256,
        total=after(values, q10),
    )
    value = q10 + after(q11, value_heads)

    raw = value.reshape(4, STEPS, 32, HD)
    norm = raw * lax.rsqrt(jnp.mean(raw * raw, axis=-1, keepdims=True) + EPS)
    gain = lax.dynamic_slice_in_dim(q_gain.reshape(HEADS, HD), core * 32, 32, 0)
    queries = (norm * gain * HD ** (-0.5)).astype(BF16)
    queries = queries.reshape(2, 2 * STEPS, 4, 8, HD).transpose(0, 2, 1, 3, 4).reshape(2, 4, 48, HD)
    queries = jnp.where(core == 0, queries, queries[::-1])
    limits = lax.dynamic_slice_in_dim(tile_counts, (yh * 4 + z) * 2, 2)
    limits = jnp.where(core == 0, limits, limits[::-1])
    usable = (jnp.arange(800, dtype=jnp.int32) // 200)[None, :] < limits[:, None]

    keys = keys.reshape(2, 800, 4, HD)
    scores = jnp.einsum("ikrd,itkd->ikrt", queries, keys, preferred_element_type=F32)
    scores = jnp.where(usable[:, None, None, :], scores, -jnp.inf)
    peak = jnp.max(scores, axis=-1, keepdims=True)
    expo = jnp.exp(scores - peak)
    total = jnp.sum(expo, axis=-1, keepdims=True)
    probs = (expo / total).astype(BF16)
    weight = (peak + jnp.log(total))[..., 0]
    high = lax.reduce_precision(weight, 8, 7)
    middle = lax.reduce_precision(weight - high, 8, 7)
    low = lax.reduce_precision(weight - high - middle, 8, 7)
    weight = jnp.stack([high, middle, low], axis=-1)
    weight = jnp.pad(weight, ((0, 0),) * 3 + ((0, HD - 3),))
    value_heads = value_heads.reshape(2, 800, 4, HD)
    part = jnp.einsum("ikrt,itkd->ikrd", probs, value_heads, preferred_element_type=F32)
    part = jnp.concatenate([part, weight], axis=2).astype(BF16)
    part = jnp.where(core == 0, part, part[::-1]).transpose(1, 0, 2, 3)
    got = lax.all_to_all(cat(part, part), ("x", "yl"), 0, 0, tiled=True)
    got = got.astype(F32)
    weight = jnp.sum(got[:, :, 48:, :3], axis=-1, keepdims=True)
    weight = jnp.exp(weight - jnp.max(weight, axis=0, keepdims=True))
    weight = weight / jnp.sum(weight, axis=0, keepdims=True)
    attention = jnp.sum(got[:, :, :48] * weight, axis=0).astype(BF16)
    spread = jnp.broadcast_to(attention[None], (16,) + attention.shape)
    got = lax.all_to_all(spread, ("yh", "z", "c"), 0, 0, tiled=True)
    got = got.reshape((8, 2) + attention.shape)
    attention = jnp.where(x < 2, got[:, 0], got[:, 1])
    attention = attention.reshape(96, 1024)
    terms = jnp.dot(attention, o_weight, preferred_element_type=F32).reshape(32, STEPS, 512)
    terms = jnp.take(terms, slot_of, axis=0).reshape(8, 4, STEPS, 512)
    got = lax.all_to_all(terms, ("x", "yl"), 0, 0, tiled=True)
    return jnp.sum(got, axis=0).transpose(1, 0, 2)


def solution(mesh):
    inner = Mesh(mesh.devices.reshape(SIZES), AXES)
    img, head = ("yh", "z", "c"), ("x", "yl")
    placed = (
        P(None, None, img + head),
        P(img, None, head, None),
        P(),
        P(),
        P(img + head, None),
        P(),
        P(img, None),
        P(img, None),
        P(head, img),
    )
    return jax.shard_map(
        per_device, mesh=inner, in_specs=placed, out_specs=P(None, head, img), check_vma=False
    )
```

time: 523 us -> 197 us (0.38)
  waiting for transfers between devices: 348 us -> 37.6 us
  blocking collectives: 80.5 us -> 19.4 us
  Pallas kernels: 0 us -> 50.7 us
  matrix products: 46.8 us -> 4.53 us
  starting transfers between devices: 0.17 us -> 39.4 us
  other arithmetic: 10.4 us -> 26 us
  between operations: 15.6 us -> 0.76 us
    psum x1 -> x0, waiting for transfers between devices: 278 us -> none  [per_device(): all_query = lax.psum(partial_value, ('img', 'head'))]
    all_gather x3 -> x0, blocking collectives: 80.5 us -> none  [the longest x2 56.9 us: combined_all(): pieces = jax.tree.map(lambda part: lax.all_gather(part, axis), value)]
    unnamed x6 -> x0, waiting for transfers between devices: 69 us -> none
    pallas_call x0 -> x3, Pallas kernels: none -> 50.7 us  [the longest x2 26.6 us: project(): pl.pallas_call(body, grid_spec=pltpu.PrefetchScalarGridSpec(num_scalar_pr...]
    dot_general x6 -> x5, matrix products: 46.8 us -> 4.53 us  [the longest x1 1.53 us: per_device(): jnp.dot(after(others, give), column_half(q_weight, 1 - core, 4096), prefe...]
    ppermute x0 -> x23, starting transfers between devices: none -> 34.5 us  [send(): return lax.ppermute(value, AXES, moves)]
    ppermute x0 -> x23, waiting for transfers between devices: none -> 26.7 us  [send(): return lax.ppermute(value, AXES, moves)]
    all_to_all x0 -> x2, blocking collectives: none -> 19.4 us  [the longest x1 10.2 us: per_device(): got = lax.all_to_all(cat(part, part), ('x', 'yl'), 0, 0, tiled=True)]
  transfers between devices with their start and end apart: 5 -> 24, of which waited for: 2 -> 8; matrix products, arithmetic and copies ran while one was open for 8% -> 17% of each run, Pallas kernels for 0% -> 26%
where the time goes in v1:
time: 197 us; the launch traced here: 196 us
  Pallas kernels  50.7 us (26%)
  starting transfers between devices  39.4 us (20%)
  waiting for transfers between devices  37.6 us (19%)
  other arithmetic  26 us (13%)
  blocking collectives  19.4 us (10%)
  local copies, waits for them, and re-layouts  17.8 us (9%)
  matrix products  4.53 us (2%)
    ppermute x23, starting transfers between devices, send(): return lax.ppermute(value, AXES, moves)  34.5 us
    ppermute x23, waiting for transfers between devices, send(): return lax.ppermute(value, AXES, moves)  26.7 us
    pallas_call x2, Pallas kernels, project(): pl.pallas_call(body, grid_spec=pltpu.PrefetchScalarGridSpec(num_scalar_pr...  26.6 us
    pallas_call x1, Pallas kernels, project_keys(): pl.pallas_call(body, grid_spec=pltpu.PrefetchScalarGridSpec(num_scalar_pr...  24.2 us
    concatenate x10, other arithmetic, cat(): return jnp.concatenate(parts, axis=0)  15.4 us
    all_to_all x1, waiting for transfers between devices, per_device(): got = lax.all_to_all(spread, ('yh', 'z', 'c'), 0, 0, tiled=True)  10.9 us
    all_to_all x1, blocking collectives, per_device(): got = lax.all_to_all(cat(part, part), ('x', 'yl'), 0, 0, tiled=True)  10.2 us
    all_to_all x1, blocking collectives, per_device(): got = lax.all_to_all(terms, ('x', 'yl'), 0, 0, tiled=True)  9.2 us
  transfers between devices with their start and end apart: 24, of which 8 were waited for; matrix products, arithmetic and copies ran while one was open for 17% of the time, Pallas kernels for 26%

profile of v1, /device:TPU:0, one launch (start us, length us, event | category | flops | bytes accessed | tf_op | source)
XLA Modules:
  0.0 196.2 jit_solution(15733957287709140262)
XLA Ops:
  10.4 2.1 %collective-permute-start.3 = (bf16[512,256]{1,0:T(8,128)(2,1)S(1)}, bf16[512,256]{1,0:T(8,128)(2,1)S(1)}, u32[]{:S(2)}, u32[]{:S(2)}) collective-permute-start(bf16[512,256]{1,0:T(8,128)(2,1)S(1)} %get-tuple-element.68), channel_id=1, source_target_pairs={{0,16},{2,18},{4,20},{6,22},{8,56},{10,58},{12,60},{14,62},{16,0},... | collective-permute-start | bytes 786440 | tf_op jit(solution)/shard_map/ppermute | solution.py:63
  13.7 1.7 dynamic-slice_select_fusion.1
  15.4 3.0 %collective-permute-start.2 = (bf16[256,512]{1,0:T(8,128)(2,1)}, bf16[256,512]{1,0:T(8,128)(2,1)S(1)}, u32[]{:S(2)}, u32[]{:S(2)}) collective-permute-start(bf16[256,512]{1,0:T(8,128)(2,1)} %dynamic-slice_select_fusion.1), channel_id=1, source_target_pairs={{0,65},{2,67},{4,69},{6,71},{8,73},{10,75},{12,77},{14,79},{16,81}... | collective-permute-start | bytes 786440 | tf_op jit(solution)/shard_map/ppermute | solution.py:63
  19.3 2.5 %collective-permute-start.5 = (bf16[1024,256]{1,0:T(8,128)(2,1)}, bf16[1024,256]{1,0:T(8,128)(2,1)}, u32[]{:S(2)}, u32[]{:S(2)}) collective-permute-start(bf16[1024,256]{1,0:T(8,128)(2,1)} %pad_maximum_fusion.7), channel_id=1, source_target_pairs={{0,48},{2,50},{4,52},{6,54},{8,24},{10,26},{12,28},{14,30},{16,32}... | collective-permute-start | bytes 1572872 | tf_op jit(solution)/shard_map/ppermute | solution.py:63
  24.5 1.9 pad_maximum_fusion.8
  26.9 3.3 %collective-permute-start.8 = (bf16[1024,256]{1,0:T(8,128)(2,1)}, bf16[1024,256]{1,0:T(8,128)(2,1)}, u32[]{:S(2)}, u32[]{:S(2)}) collective-permute-start(bf16[1024,256]{1,0:T(8,128)(2,1)} %pad_maximum_fusion.6), channel_id=1, source_target_pairs={{0,65},{2,67},{4,69},{6,71},{8,73},{10,75},{12,77},{14,79},{16,81}... | collective-permute-start | bytes 1572872 | tf_op jit(solution)/shard_map/ppermute | solution.py:63
  31.3 2.1 %pad_maximum_fusion.3 = bf16[2048,256]{1,0:T(8,128)(2,1)} fusion(bf16[1024,256]{1,0:T(8,128)(2,1)} %collective-permute-done.5, bf16[512,256]{1,0:T(8,128)(2,1)S(1)} %copy-done.10, bf16[512,256]{1,0:T(8,128)(2,1)S(1)} %copy-done.7), kind=kLoop, calls=%fused_computation.18 | loop fusion | flops 3145728 | bytes 2097152 | tf_op jit(solution)/shard_map/concatenate | solution.py:67
  33.3 2.6 %collective-permute-done.4 = bf16[512,512]{1,0:T(8,128)(2,1)} collective-permute-done((bf16[512,512]{1,0:T(8,128)(2,1)}, bf16[512,512]{1,0:T(8,128)(2,1)}, u32[]{:S(2)}, u32[]{:S(2)}) %collective-permute-start.4) | collective-permute-done | bytes 524320 | tf_op jit(solution)/shard_map/ppermute | solution.py:63
  37.1 1.6 collective-permute-start.9
  38.6 2.2 %pad_maximum_fusion.4 = bf16[1024,512]{1,0:T(8,128)(2,1)} fusion(bf16[512,512]{1,0:T(8,128)(2,1)} %collective-permute-done.4, bf16[256,512]{1,0:T(8,128)(2,1)S(1)} %copy-done.13, bf16[256,512]{1,0:T(8,128)(2,1)} %dynamic-slice_select_fusion.1), kind=kLoop, calls=%fused_computation.19 | loop fusion | flops 3145728 | bytes 2097152 | tf_op jit(solution)/shard_map/concatenate | solution.py:67
  40.8 3.2 %collective-permute-start.7 = (bf16[1024,512]{1,0:T(8,128)(2,1)}, bf16[1024,512]{1,0:T(8,128)(2,1)S(1)}, u32[]{:S(2)}, u32[]{:S(2)}) collective-permute-start(bf16[1024,512]{1,0:T(8,128)(2,1)} %pad_maximum_fusion.4), channel_id=1, source_target_pairs={{0,48},{2,50},{4,52},{6,54},{8,24},{10,26},{12,28},{14,30},{16,32}... | collective-permute-start | bytes 3145736 | tf_op jit(solution)/shard_map/ppermute | solution.py:63
  44.1 2.1 %slice_add_fusion = f32[48,4096]{1,0:T(8,128)} fusion(f32[48,4096]{1,0:T(8,128)S(1)} %slice-done, f32[96,4096]{1,0:T(8,128)} %collective-permute-done), kind=kLoop, calls=%fused_computation.23 | loop fusion | flops 196608 | bytes 2359296 | tf_op jit(solution)/shard_map/add | solution.py:306
  46.7 2.5 %collective-permute-done.9.refs_13_ = bf16[768,512]{1,0:T(8,128)(2,1)} collective-permute-done((bf16[768,512]{1,0:T(8,128)(2,1)S(1)}, bf16[768,512]{1,0:T(8,128)(2,1)}, u32[]{:S(2)}, u32[]{:S(2)}) %collective-permute-start.9) | collective-permute-done | bytes 786464 | tf_op jit(solution)/shard_map/ppermute | solution.py:63
  49.7 2.1 %constant_dynamic-update-slice_fusion.2 = bf16[1536,512]{1,0:T(8,128)(2,1)} fusion(bf16[1536,512]{1,0:T(8,128)(2,1)} %copy-done.16, bf16[768,512]{1,0:T(8,128)(2,1)} %collective-permute-done.9.refs_13_), kind=kLoop, calls=%fused_computation.69 | loop fusion | bytes 1572864 | tf_op jit(solution)/shard_map/concatenate | solution.py:67
  51.8 2.8 %collective-permute-start.16 = (bf16[1536,512]{1,0:T(8,128)(2,1)}, bf16[1536,512]{1,0:T(8,128)(2,1)S(1)}, u32[]{:S(2)}, u32[]{:S(2)}) collective-permute-start(bf16[1536,512]{1,0:T(8,128)(2,1)} %constant_dynamic-update-slice_fusion.2), channel_id=1, source_target_pairs={{0,6},{2,4},{4,2},{6,0},{8,10},{10,8},{12,14},{14,12},{16,22},{18,... | collective-permute-start | bytes 4718600 | tf_op jit(solution)/shard_map/ppermute | solution.py:63
  56.2 9.7 %collective-permute-done.7.refs_8_ = bf16[1024,512]{1,0:T(8,128)(2,1)S(1)} collective-permute-done((bf16[1024,512]{1,0:T(8,128)(2,1)}, bf16[1024,512]{1,0:T(8,128)(2,1)S(1)}, u32[]{:S(2)}, u32[]{:S(2)}) %collective-permute-start.7) | collective-permute-done | bytes 1048608 | tf_op jit(solution)/shard_map/ppermute | solution.py:63
  68.2 3.1 %collective-permute-start.11 = (f32[24,4096]{1,0:T(8,128)S(1)}, f32[24,4096]{1,0:T(8,128)S(1)}, u32[]{:S(2)}, u32[]{:S(2)}) collective-permute-start(f32[24,4096]{1,0:T(8,128)S(1)} %slice.86), channel_id=1, source_target_pairs={{0,65},{2,67},{4,69},{6,71},{8,73},{10,75},{12,77},{14,79},{16,81}... | collective-permute-start | bytes 1179656 | tf_op jit(solution)/shard_map/ppermute | solution.py:63
  71.4 2.5 %pad_maximum_fusion.l0 = bf16[4096,256]{1,0:T(8,128)(2,1)} fusion(bf16[2048,256]{1,0:T(8,128)(2,1)S(1)} %collective-permute-done.12, bf16[1024,256]{1,0:T(8,128)(2,1)} %collective-permute-done.5, bf16[512,256]{1,0:T(8,128)(2,1)S(1)} %copy-done.11, bf16[512,256]{1,0:T(8,128)(2,1)S(1)} %copy-done.8), kind=kLoop, calls=%fused_computation.5 | loop fusion | flops 8388608 | bytes 4194304 | tf_op jit(solution)/shard_map/concatenate | solution.py:67
  75.1 4.9 %collective-permute-done.11 = f32[24,4096]{1,0:T(8,128)S(1)} collective-permute-done((f32[24,4096]{1,0:T(8,128)S(1)}, f32[24,4096]{1,0:T(8,128)S(1)}, u32[]{:S(2)}, u32[]{:S(2)}) %collective-permute-start.11) | collective-permute-done | bytes 393248 | tf_op jit(solution)/shard_map/ppermute | solution.py:63
  80.1 2.0 collective-permute-start.13
  82.0 2.5 %pad_maximum_fusion.1.u0 = bf16[4096,256]{1,0:T(8,128)(2,1)} fusion(bf16[2048,256]{1,0:T(8,128)(2,1)S(1)} %collective-permute-done.14, bf16[1024,256]{1,0:T(8,128)(2,1)} %collective-permute-done.8, bf16[512,256]{1,0:T(8,128)(2,1)S(1)} %get-tuple-element.69, bf16[512,256]{1,0:T(8,128)(2,1)S(1)} %get-tuple-element.67), kind=kLoop, calls=%fused_computation.6 | loop fusion | flops 8388608 | bytes 4194304 | tf_op jit(solution)/shard_map/concatenate | solution.py:67
  85.9 1.8 collective-permute-done.13
  89.2 12.9 %shard_map.91.refs_12_ = f32[2,800,512]{2,1,0:T(8,128)} custom-call(s32[16]{0:T(128)S(1)} %stack.472.idx_ref, bf16[800,8192]{1,0:T(8,128)(2,1)} %bitcast.190, bf16[800,8192]{1,0:T(8,128)(2,1)} %collective-permute-done.10.refs_1_.refs_3_.refs_5_.refs_7_.t_ref, bf16[800,8192]{1,0:T(8,128)(2,1)} %bitcast.191, ...), custom_call_target="tpu_custom_call" | custom-call | flops 6710886400 | bytes 13107200 | tf_op jit(solution)/shard_map/pallas_call | solution.py:148
  104.3 3.0 %collective-permute-start.22 = (bf16[2048,512]{1,0:T(8,128)(2,1)}, bf16[2048,512]{1,0:T(8,128)(2,1)}, u32[]{:S(2)}, u32[]{:S(2)}) collective-permute-start(bf16[2048,512]{1,0:T(8,128)(2,1)} %constant_dynamic-update-slice_fusion.5), channel_id=1, source_target_pairs={{0,6},{2,4},{4,2},{6,0},{8,10},{10,8},{12,14},{14,12},{16,22},{18,... | collective-permute-start | bytes 6291464 | tf_op jit(solution)/shard_map/ppermute | solution.py:63
  108.1 4.0 %collective-permute-done.20.u1 = bf16[4096,256]{1,0:T(8,128)(2,1)} collective-permute-done((bf16[4096,256]{1,0:T(8,128)(2,1)}, bf16[4096,256]{1,0:T(8,128)(2,1)}, u32[]{:S(2)}, u32[]{:S(2)}) %collective-permute-start.20) | collective-permute-done | bytes 2097184 | tf_op jit(solution)/shard_map/ppermute | solution.py:63
  112.1 24.2 %shard_map.92 = bf16[2,800,512]{2,1,0:T(8,128)(2,1)S(1)} custom-call(s32[48]{0:T(128)S(1)} %reshape.197.idx_ref, bf16[800,8192]{1,0:T(8,128)(2,1)} %bitcast.194, bf16[800,8192]{1,0:T(8,128)(2,1)} %collective-permute-done.10.refs_1_.refs_3_.refs_5_.refs_7_.t_ref, bf16[4096,256]{1,0:T(8,128)(2,1)} %pad_maximum_fusion.l0, ...), custom_call_target="tpu_custom_call" | custom-call | flops 13421772800 | bytes 26214400 | tf_op jit(solution)/shard_map/pallas_call | solution.py:213
  136.3 3.5 %collective-permute-start.21 = (f32[12,4096]{1,0:T(8,128)S(1)}, f32[12,4096]{1,0:T(8,128)S(1)}, u32[]{:S(2)}, u32[]{:S(2)}) collective-permute-start(f32[12,4096]{1,0:T(8,128)S(1)} %add.773), channel_id=1, source_target_pairs={{0,6},{2,4},{4,2},{6,0},{8,10},{10,8},{12,14},{14,12},{16,22},{18,... | collective-permute-start | bytes 589832 | tf_op jit(solution)/shard_map/ppermute | solution.py:63
  139.9 13.7 %shard_map.93 = bf16[2,800,512]{2,1,0:T(8,128)(2,1)} custom-call(s32[16]{0:T(128)S(1)} %stack.546.idx_ref, bf16[800,8192]{1,0:T(8,128)(2,1)} %bitcast.195, bf16[800,8192]{1,0:T(8,128)(2,1)} %collective-permute-done.10.refs_1_.refs_3_.refs_5_.refs_7_.t_ref, bf16[800,8192]{1,0:T(8,128)(2,1)} %bitcast.196, ...), custom_call_target="tpu_custom_call" | custom-call | flops 6710886400 | bytes 13107200 | tf_op jit(solution)/shard_map/pallas_call | solution.py:148
  157.5 10.2 %all_to_all.15 = bf16[8,2,96,128]{3,2,1,0:T(8,128)(2,1)S(1)} all-to-all(bf16[8,2,96,128]{3,2,1,0:T(8,128)(2,1)S(1)} %copy.84), channel_id=1, replica_groups=mesh['yh'=2,'z'=4,'c'=2,'x'=4,'yl'=2] {'x','yl'}, dimensions={0} | all-to-all | bytes 786432 | tf_op jit(solution)/shard_map/all_to_all | solution.py:398
  169.0 5.0 %all-to-all-start.1 = ((bf16[16,2,48,128]{3,2,1,0:T(8,128)(2,1)}), bf16[16,2,48,128]{3,2,1,0:T(8,128)(2,1)S(1)}, u32[]{:S(2)}, u32[]{:S(2)}) async-start(bf16[16,2,48,128]{3,2,1,0:T(8,128)(2,1)} %broadcast_in_dim.79), calls=%async_computation.1 | async-start | bytes 786432 | tf_op jit(solution)/shard_map/all_to_all | solution.py:405
  174.1 10.9 %all-to-all-done.1 = bf16[16,2,48,128]{3,2,1,0:T(8,128)(2,1)S(1)} async-done(((bf16[16,2,48,128]{3,2,1,0:T(8,128)(2,1)}), bf16[16,2,48,128]{3,2,1,0:T(8,128)(2,1)S(1)}, u32[]{:S(2)}, u32[]{:S(2)}) %all-to-all-start.1) | async-done | bytes 393248 | tf_op jit(solution)/shard_map/all_to_all | solution.py:405
  186.4 9.2 %all_to_all.16 = f32[8,4,3,512]{3,1,2,0:T(4,128)S(1)} all-to-all(f32[8,4,3,512]{3,1,2,0:T(4,128)S(1)} %copy_select_fusion), channel_id=1, replica_groups=mesh['yh'=2,'z'=4,'c'=2,'x'=4,'yl'=2] {'x','yl'}, dimensions={0} | all-to-all | bytes 393216 | tf_op jit(solution)/shard_map/all_to_all | solution.py:411
  (170 shorter events, 36.9 us)
Async XLA Ops:
  2.6 3.7 %collective-permute-start.1 = (bf16[1024,512]{1,0:T(8,128)(2,1)}, bf16[1024,512]{1,0:T(8,128)(2,1)}, u32[]{:S(2)}, u32[]{:S(2)}) collective-permute-start(bf16[1024,512]{1,0:T(8,128)(2,1)} %pad_maximum_fusion.2), channel_id=1, source_target_pairs={{0,8},{2,10},{4,12},{6,14},{8,0},{10,2},{12,4},{14,6},{16,24},{18,... | collective-permute-start | bytes 3145736 | tf_op jit(solution)/shard_map/ppermute | solution.py:63
  7.6 11.8 %copy-start.6 = (bf16[512,256]{1,0:T(8,128)(2,1)}, bf16[512,256]{1,0:T(8,128)(2,1)S(1)}, u32[]{:S(2)}) copy-start(bf16[512,256]{1,0:T(8,128)(2,1)S(1)} %get-tuple-element.68) | copy-start | bytes 786436
  8.5 41.2 %collective-permute-start.10 = (bf16[800,8192]{1,0:T(8,128)(2,1)}, bf16[800,8192]{1,0:T(8,128)(2,1)}, u32[]{:S(2)}, u32[]{:S(2)}) collective-permute-start(bf16[800,8192]{1,0:T(8,128)(2,1)} %bitcast.189), channel_id=1, source_target_pairs={{0,8},{2,10},{4,12},{6,14},{8,0},{10,2},{12,4},{14,6},{16,24},{18,... | collective-permute-start | bytes 39321608 | tf_op jit(solution)/shard_map/ppermute | solution.py:63
  9.0 35.1 %collective-permute-start = (f32[96,4096]{1,0:T(8,128)}, f32[96,4096]{1,0:T(8,128)}, u32[]{:S(2)}, u32[]{:S(2)}) collective-permute-start(f32[96,4096]{1,0:T(8,128)} %fusion.18), channel_id=1, source_target_pairs={{0,8},{2,10},{4,12},{6,14},{8,0},{10,2},{12,4},{14,6},{16,24},{18,... | collective-permute-start | bytes 4718600 | tf_op jit(solution)/shard_map/ppermute | solution.py:63
  10.4 8.0 %collective-permute-start.3 = (bf16[512,256]{1,0:T(8,128)(2,1)S(1)}, bf16[512,256]{1,0:T(8,128)(2,1)S(1)}, u32[]{:S(2)}, u32[]{:S(2)}) collective-permute-start(bf16[512,256]{1,0:T(8,128)(2,1)S(1)} %get-tuple-element.68), channel_id=1, source_target_pairs={{0,16},{2,18},{4,20},{6,22},{8,56},{10,58},{12,60},{14,62},{16,0},... | collective-permute-start | bytes 786440 | tf_op jit(solution)/shard_map/ppermute | solution.py:63
  15.4 9.1 %collective-permute-start.2 = (bf16[256,512]{1,0:T(8,128)(2,1)}, bf16[256,512]{1,0:T(8,128)(2,1)S(1)}, u32[]{:S(2)}, u32[]{:S(2)}) collective-permute-start(bf16[256,512]{1,0:T(8,128)(2,1)} %dynamic-slice_select_fusion.1), channel_id=1, source_target_pairs={{0,65},{2,67},{4,69},{6,71},{8,73},{10,75},{12,77},{14,79},{16,81}... | collective-permute-start | bytes 786440 | tf_op jit(solution)/shard_map/ppermute | solution.py:63
  19.3 11.9 %collective-permute-start.5 = (bf16[1024,256]{1,0:T(8,128)(2,1)}, bf16[1024,256]{1,0:T(8,128)(2,1)}, u32[]{:S(2)}, u32[]{:S(2)}) collective-permute-start(bf16[1024,256]{1,0:T(8,128)(2,1)} %pad_maximum_fusion.7), channel_id=1, source_target_pairs={{0,48},{2,50},{4,52},{6,54},{8,24},{10,26},{12,28},{14,30},{16,32}... | collective-permute-start | bytes 1572872 | tf_op jit(solution)/shard_map/ppermute | solution.py:63
  26.5 9.5 %collective-permute-start.4 = (bf16[512,512]{1,0:T(8,128)(2,1)}, bf16[512,512]{1,0:T(8,128)(2,1)}, u32[]{:S(2)}, u32[]{:S(2)}) collective-permute-start(bf16[512,512]{1,0:T(8,128)(2,1)} %pad_maximum_fusion.8), channel_id=1, source_target_pairs={{0,16},{2,18},{4,20},{6,22},{8,56},{10,58},{12,60},{14,62},{16,0},... | collective-permute-start | bytes 1572872 | tf_op jit(solution)/shard_map/ppermute | solution.py:63
  26.9 27.7 %collective-permute-start.8 = (bf16[1024,256]{1,0:T(8,128)(2,1)}, bf16[1024,256]{1,0:T(8,128)(2,1)}, u32[]{:S(2)}, u32[]{:S(2)}) collective-permute-start(bf16[1024,256]{1,0:T(8,128)(2,1)} %pad_maximum_fusion.6), channel_id=1, source_target_pairs={{0,65},{2,67},{4,69},{6,71},{8,73},{10,75},{12,77},{14,79},{16,81}... | collective-permute-start | bytes 1572872 | tf_op jit(solution)/shard_map/ppermute | solution.py:63
  33.3 10.7 %slice-start = ((f32[96,4096]{1,0:T(8,128)}), f32[48,4096]{1,0:T(8,128)S(1)}, s32[]{:S(2)}) async-start(f32[96,4096]{1,0:T(8,128)} %fusion.20), calls=%async_computation.3 | async-start | bytes 1572864 | tf_op jit(solution)/shard_map/slice | solution.py:306
  37.1 9.1 %copy-start.16 = (bf16[1536,512]{1,0:T(8,128)(2,1)}, bf16[1536,512]{1,0:T(8,128)(2,1)S(1)}, u32[]{:S(2)}) copy-start(bf16[1536,512]{1,0:T(8,128)(2,1)S(1)} %get-tuple-element.70) | copy-start | bytes 4718596
  37.1 12.2 %collective-permute-start.9 = (bf16[768,512]{1,0:T(8,128)(2,1)S(1)}, bf16[768,512]{1,0:T(8,128)(2,1)}, u32[]{:S(2)}, u32[]{:S(2)}) collective-permute-start(bf16[768,512]{1,0:T(8,128)(2,1)S(1)} %get-tuple-element.71.refs_12_), channel_id=1, source_target_pairs={{0,2},{2,0},{4,6},{6,4},{8,14},{10,12},{12,10},{14,8},{16,18},{18,... | collective-permute-start | bytes 2359304 | tf_op jit(solution)/shard_map/ppermute | solution.py:63
  40.8 25.1 %collective-permute-start.7 = (bf16[1024,512]{1,0:T(8,128)(2,1)}, bf16[1024,512]{1,0:T(8,128)(2,1)S(1)}, u32[]{:S(2)}, u32[]{:S(2)}) collective-permute-start(bf16[1024,512]{1,0:T(8,128)(2,1)} %pad_maximum_fusion.4), channel_id=1, source_target_pairs={{0,48},{2,50},{4,52},{6,54},{8,24},{10,26},{12,28},{14,30},{16,32}... | collective-permute-start | bytes 3145736 | tf_op jit(solution)/shard_map/ppermute | solution.py:63
  46.2 20.5 %collective-permute-start.6 = (f32[48,4096]{1,0:T(8,128)}, f32[48,4096]{1,0:T(8,128)}, u32[]{:S(2)}, u32[]{:S(2)}) collective-permute-start(f32[48,4096]{1,0:T(8,128)} %slice_add_fusion), channel_id=1, source_target_pairs={{0,16},{2,18},{4,20},{6,22},{8,56},{10,58},{12,60},{14,62},{16,0},... | collective-permute-start | bytes 2359304 | tf_op jit(solution)/shard_map/ppermute | solution.py:63
  46.5 20.2 %copy-start.3 = (f32[96,4096]{1,0:T(8,128)S(1)}, f32[96,4096]{1,0:T(8,128)}, u32[]{:S(2)}) copy-start(f32[96,4096]{1,0:T(8,128)} %fusion.20) | copy-start | bytes 4718596
  49.2 19.0 %collective-permute-start.12 = (bf16[2048,256]{1,0:T(8,128)(2,1)}, bf16[2048,256]{1,0:T(8,128)(2,1)S(1)}, u32[]{:S(2)}, u32[]{:S(2)}) collective-permute-start(bf16[2048,256]{1,0:T(8,128)(2,1)} %pad_maximum_fusion.3), channel_id=1, source_target_pairs={{0,1},{2,3},{4,5},{6,7},{8,73},{10,75},{12,77},{14,79},{16,17},{18... | collective-permute-start | bytes 3145736 | tf_op jit(solution)/shard_map/ppermute | solution.py:63
  51.8 36.3 %collective-permute-start.16 = (bf16[1536,512]{1,0:T(8,128)(2,1)}, bf16[1536,512]{1,0:T(8,128)(2,1)S(1)}, u32[]{:S(2)}, u32[]{:S(2)}) collective-permute-start(bf16[1536,512]{1,0:T(8,128)(2,1)} %constant_dynamic-update-slice_fusion.2), channel_id=1, source_target_pairs={{0,6},{2,4},{4,2},{6,0},{8,10},{10,8},{12,14},{14,12},{16,22},{18,... | collective-permute-start | bytes 4718600 | tf_op jit(solution)/shard_map/ppermute | solution.py:63
  55.7 15.7 %copy-start.8 = (bf16[512,256]{1,0:T(8,128)(2,1)S(1)}, bf16[512,256]{1,0:T(8,128)(2,1)}, u32[]{:S(2)}) copy-start(bf16[512,256]{1,0:T(8,128)(2,1)} %copy-done.6) | copy-start | bytes 786436
  55.7 15.7 %copy-start.11 = (bf16[512,256]{1,0:T(8,128)(2,1)S(1)}, bf16[512,256]{1,0:T(8,128)(2,1)}, u32[]{:S(2)}) copy-start(bf16[512,256]{1,0:T(8,128)(2,1)} %copy-done.9) | copy-start | bytes 786436
  55.7 26.4 %collective-permute-start.14 = (bf16[2048,256]{1,0:T(8,128)(2,1)S(1)}, bf16[2048,256]{1,0:T(8,128)(2,1)S(1)}, u32[]{:S(2)}, u32[]{:S(2)}) collective-permute-start(bf16[2048,256]{1,0:T(8,128)(2,1)S(1)} %pad_maximum_fusion.5), channel_id=1, source_target_pairs={{0,16},{2,18},{4,20},{6,22},{8,56},{10,58},{12,60},{14,62},{16,0},... | collective-permute-start | bytes 3145736 | tf_op jit(solution)/shard_map/ppermute | solution.py:63
  65.9 36.3 %collective-permute-start.19 = (bf16[1024,512]{1,0:T(8,128)(2,1)S(1)}, bf16[1024,512]{1,0:T(8,128)(2,1)S(1)}, u32[]{:S(2)}, u32[]{:S(2)}) collective-permute-start(bf16[1024,512]{1,0:T(8,128)(2,1)S(1)} %collective-permute-done.7.refs_8_), channel_id=1, source_target_pairs={{0,2},{2,0},{4,6},{6,4},{8,14},{10,12},{12,10},{14,8},{16,18},{18,... | collective-permute-start | bytes 3145736 | tf_op jit(solution)/shard_map/ppermute | solution.py:63
  68.2 11.8 %collective-permute-start.11 = (f32[24,4096]{1,0:T(8,128)S(1)}, f32[24,4096]{1,0:T(8,128)S(1)}, u32[]{:S(2)}, u32[]{:S(2)}) collective-permute-start(f32[24,4096]{1,0:T(8,128)S(1)} %slice.86), channel_id=1, source_target_pairs={{0,65},{2,67},{4,69},{6,71},{8,73},{10,75},{12,77},{14,79},{16,81}... | collective-permute-start | bytes 1179656 | tf_op jit(solution)/shard_map/ppermute | solution.py:63
  73.9 34.3 %collective-permute-start.18 = (bf16[4096,256]{1,0:T(8,128)(2,1)}, bf16[4096,256]{1,0:T(8,128)(2,1)}, u32[]{:S(2)}, u32[]{:S(2)}) collective-permute-start(bf16[4096,256]{1,0:T(8,128)(2,1)} %pad_maximum_fusion.l0), channel_id=1, source_target_pairs={{0,65},{2,67},{4,69},{6,71},{8,9},{10,11},{12,13},{14,15},{16,81},... | collective-permute-start | bytes 6291464 | tf_op jit(solution)/shard_map/ppermute | solution.py:63
  80.1 7.7 %collective-permute-start.13 = (f32[12,4096]{1,0:T(8,128)S(1)}, f32[12,4096]{1,0:T(8,128)S(1)}, u32[]{:S(2)}, u32[]{:S(2)}) collective-permute-start(f32[12,4096]{1,0:T(8,128)S(1)} %slice.88), channel_id=1, source_target_pairs={{0,48},{2,50},{4,52},{6,54},{8,24},{10,26},{12,28},{14,30},{16,32}... | collective-permute-start | bytes 589832 | tf_op jit(solution)/shard_map/ppermute | solution.py:63
  84.5 27.6 %collective-permute-start.20 = (bf16[4096,256]{1,0:T(8,128)(2,1)}, bf16[4096,256]{1,0:T(8,128)(2,1)}, u32[]{:S(2)}, u32[]{:S(2)}) collective-permute-start(bf16[4096,256]{1,0:T(8,128)(2,1)} %pad_maximum_fusion.1.u0), channel_id=1, source_target_pairs={{0,48},{2,50},{4,52},{6,54},{8,24},{10,26},{12,28},{14,30},{16,32}... | collective-permute-start | bytes 6291464 | tf_op jit(solution)/shard_map/ppermute | solution.py:63
  87.8 14.4 %collective-permute-start.15 = (f32[12,4096]{1,0:T(8,128)S(1)}, f32[12,4096]{1,0:T(8,128)S(1)}, u32[]{:S(2)}, u32[]{:S(2)}) collective-permute-start(f32[12,4096]{1,0:T(8,128)S(1)} %slice_add_fusion.3), channel_id=1, source_target_pairs={{0,1},{2,3},{4,5},{6,7},{8,9},{10,11},{12,13},{14,15},{16,17},{18,... | collective-permute-start | bytes 589832 | tf_op jit(solution)/shard_map/ppermute | solution.py:63
  104.3 35.5 %collective-permute-start.22 = (bf16[2048,512]{1,0:T(8,128)(2,1)}, bf16[2048,512]{1,0:T(8,128)(2,1)}, u32[]{:S(2)}, u32[]{:S(2)}) collective-permute-start(bf16[2048,512]{1,0:T(8,128)(2,1)} %constant_dynamic-update-slice_fusion.5), channel_id=1, source_target_pairs={{0,6},{2,4},{4,2},{6,0},{8,10},{10,8},{12,14},{14,12},{16,22},{18,... | collective-permute-start | bytes 6291464 | tf_op jit(solution)/shard_map/ppermute | solution.py:63
  108.1 28.2 %collective-permute-start.17 = (f32[12,4096]{1,0:T(8,128)S(1)}, f32[12,4096]{1,0:T(8,128)S(1)}, u32[]{:S(2)}, u32[]{:S(2)}) collective-permute-start(f32[12,4096]{1,0:T(8,128)S(1)} %add.717), channel_id=1, source_target_pairs={{0,2},{2,0},{4,6},{6,4},{8,14},{10,12},{12,10},{14,8},{16,18},{18,... | collective-permute-start | bytes 589832 | tf_op jit(solution)/shard_map/ppermute | solution.py:63
  136.3 17.2 %collective-permute-start.21 = (f32[12,4096]{1,0:T(8,128)S(1)}, f32[12,4096]{1,0:T(8,128)S(1)}, u32[]{:S(2)}, u32[]{:S(2)}) collective-permute-start(f32[12,4096]{1,0:T(8,128)S(1)} %add.773), channel_id=1, source_target_pairs={{0,6},{2,4},{4,2},{6,0},{8,10},{10,8},{12,14},{14,12},{16,22},{18,... | collective-permute-start | bytes 589832 | tf_op jit(solution)/shard_map/ppermute | solution.py:63
  167.7 17.4 %copy-start.15 = (bf16[1024,512]{1,0:T(8,128)(2,1)S(1)}, bf16[1024,512]{1,0:T(8,128)(2,1)}, u32[]{:S(2)}) copy-start(bf16[1024,512]{1,0:T(8,128)(2,1)} %param.21) | copy-start | bytes 3145732
  169.0 15.9 %all-to-all-start.1 = ((bf16[16,2,48,128]{3,2,1,0:T(8,128)(2,1)}), bf16[16,2,48,128]{3,2,1,0:T(8,128)(2,1)S(1)}, u32[]{:S(2)}, u32[]{:S(2)}) async-start(bf16[16,2,48,128]{3,2,1,0:T(8,128)(2,1)} %broadcast_in_dim.79), calls=%async_computation.1 | async-start | bytes 786432 | tf_op jit(solution)/shard_map/all_to_all | solution.py:405
  185.0 11.2 %copy-start.1 = (bf16[64,8192]{1,0:T(8,128)(2,1)S(1)}, bf16[64,8192]{1,0:T(8,128)(2,1)}, u32[]{:S(2)}) copy-start(bf16[64,8192]{1,0:T(8,128)(2,1)} %param.17) | copy-start | bytes 3145732
  (13 other events, 56.1 us)

commit v2 on v1

--- a/solution.py
+++ b/solution.py
@@ -166,39 +166,45 @@
 
 def project_keys(features, lower, upper, steps):
     tokens = features[0].shape[0]
-    size, width = 512, 256
-    count = len(steps)
+    size, width, terms = 512, 256, 2
+    count = len(steps) // terms
     table = jnp.stack([jnp.stack([jnp.asarray(n, jnp.int32) for n in s]) for s in steps])
     span = count // 4
 
-    def rows_at(column, busy):
+    def rows_at(column, busy, t):
         def at(i, idx):
             now = jnp.int32(0)
-            for g in range(4):
-                near = i - g * span
+            for g in busy:
                 use = jnp.clip(i, g * span, (g + 1) * span - 1)
-                if g in busy:
-                    now = jnp.where(
-                        jnp.logical_or(near >= 0, g == min(busy)), idx[use * 3 + column], now
-                    )
+                spot = idx[(use * terms + t) * 3 + column]
+                now = jnp.where(jnp.logical_or(i >= g * span, g == busy[0]), spot, now)
             return (now, 0)
 
         return at
 
-    def body(idx_ref, m_ref, t_ref, l0, l1, u0, u1, out_ref, acc_ref):
+    def body(idx_ref, *refs):
         step = pl.program_id(0)
+        out_ref, acc_ref = refs[-2:]
+        left, right = refs[: 2 * terms], refs[2 * terms : -2]
 
         @pl.when(step == 0)
         def _():
             acc_ref[...] = jnp.zeros_like(acc_ref)
 
-        for g, (low, up) in enumerate(((l0, u0), (l0, u1), (l1, u0), (l1, u1))):
+        for g, (low, up) in enumerate(((0, 2), (0, 3), (1, 2), (1, 3))):
 
             @pl.when(step // span == g)
             def _(low=low, up=up):
-                rows = jnp.concatenate([low[...], up[...]], axis=1)
-                acc_ref[0] += jnp.dot(m_ref[...], rows, preferred_element_type=F32)
-                acc_ref[1] += jnp.dot(t_ref[...], rows, preferred_element_type=F32)
+                rows = jnp.concatenate(
+                    [
+                        jnp.concatenate([right[4 * t + low][...], right[4 * t + up][...]], axis=1)
+                        for t in range(terms)
+                    ],
+                    axis=0,
+                )
+                for i in range(2):
+                    cols = jnp.concatenate([left[2 * t + i][...] for t in range(terms)], axis=1)
+                    acc_ref[i] += jnp.dot(cols, rows, preferred_element_type=F32)
 
         @pl.when(step == count - 1)
         def _():
@@ -208,32 +214,34 @@
                     mean = jnp.mean(part * part, axis=-1, keepdims=True)
                     out_ref[i, :, h * HD : (h + 1) * HD] = (part * lax.rsqrt(mean + EPS)).astype(BF16)
 
-    column = pl.BlockSpec((tokens, size), lambda i, idx: (0, idx[i * 3]))
+    arrays, in_specs = [], []
+    for t in range(terms):
+        arrays += features
+        in_specs += [
+            pl.BlockSpec((tokens, size), lambda i, idx, t=t: (0, idx[(i * terms + t) * 3]))
+        ] * 2
+    for t in range(terms):
+        arrays += [*lower, *upper]
+        for column, busy in ((1, (0, 1)), (1, (2, 3)), (2, (0, 2)), (2, (1, 3))):
+            in_specs.append(pl.BlockSpec((size, width), rows_at(column, busy, t)))
     shape = (2, tokens, 2 * width)
     return pl.pallas_call(
         body,
         grid_spec=pltpu.PrefetchScalarGridSpec(
             num_scalar_prefetch=1,
             grid=(count,),
-            in_specs=[
-                column,
-                column,
-                pl.BlockSpec((size, width), rows_at(1, (0, 1))),
-                pl.BlockSpec((size, width), rows_at(1, (2, 3))),
-                pl.BlockSpec((size, width), rows_at(2, (0, 2))),
-                pl.BlockSpec((size, width), rows_at(2, (1, 3))),
-            ],
+            in_specs=in_specs,
             out_specs=pl.BlockSpec(shape, lambda i, idx: (0, 0, 0)),
             scratch_shapes=[pltpu.VMEM(shape, F32)],
         ),
         out_shape=jax.ShapeDtypeStruct(shape, BF16),
         cost_estimate=pl.CostEstimate(
-            flops=8 * tokens * size * count * width,
-            bytes_accessed=4 * tokens * size * count,
+            flops=8 * tokens * size * terms * count * width,
+            bytes_accessed=4 * tokens * size * terms * count,
             transcendentals=0,
         ),
         compiler_params=pltpu.CompilerParams(vmem_limit_bytes=52 * 1024 * 1024),
-    )(table.reshape(-1), *features, *lower, *upper)
+    )(table.reshape(-1), *arrays)
 
 
 def slots(core, v):
@@ -265,22 +273,19 @@
 
     def leaving(one, two):
         zpairs = ((z, two), (one, zs[3]))
-        places = [
+        return [
             (h * 4 + zz) * 4 + k for zp in zpairs for h in (yh, 1 - yh) for zz in zp for k in range(4)
         ]
-        rows = jnp.take(hidden, jnp.take(request_at, jnp.stack(places)), axis=1)
-        return rows.transpose(1, 0, 2).reshape(96, 64)
 
     give = cat(column_half(k_weight, 1 - core, 512), column_half(v_weight, 1 - core, 512))
     got = send(give, CORE)
-    others = leaving(zs[2], zs[1])
+    places = jnp.stack(leaving(zs[2], zs[1]) + leaving(zs[1], zs[2]))
+    rows = jnp.take(hidden, jnp.take(request_at, places), axis=1)
+    rows = after(rows.transpose(1, 0, 2).reshape(192, 64), give)
     q_give = jnp.dot(
-        after(others, give), column_half(q_weight, 1 - core, 4096), preferred_element_type=F32
+        rows[:96], column_half(q_weight, 1 - core, 4096), preferred_element_type=F32
     )
     q_got = send(q_give, CORE)
-    q_mine = jnp.dot(
-        leaving(zs[1], zs[2]), column_half(q_weight, core, 4096), preferred_element_type=F32
-    )
     mine = vision.reshape(800, 8192)
     got = after(got, q_give)
     k_mine, v_mine = column_half(k_weight, core, 512), column_half(v_weight, core, 512)
@@ -292,7 +297,10 @@
     c1 = send(c0, YC)
     a1 = send(a0, Z1)
     b1 = send(after(b0, a0, c0), YC)
-    theirs = send(after(mine, b0), CORE)
+    theirs = send(after(mine, b0, a0, c0), CORE)
+    q_mine = jnp.dot(
+        after(rows, a0, c0)[96:], column_half(q_weight, core, 4096), preferred_element_type=F32
+    )
     a01 = cat(a0, after(a1, b0))
     a2 = send(a01, Z2)
     c01 = cat(c0, after(c1, a01))
@@ -401,10 +409,10 @@
     weight = jnp.exp(weight - jnp.max(weight, axis=0, keepdims=True))
     weight = weight / jnp.sum(weight, axis=0, keepdims=True)
     attention = jnp.sum(got[:, :, :48] * weight, axis=0).astype(BF16)
-    spread = jnp.broadcast_to(attention[None], (16,) + attention.shape)
-    got = lax.all_to_all(spread, ("yh", "z", "c"), 0, 0, tiled=True)
-    got = got.reshape((8, 2) + attention.shape)
-    attention = jnp.where(x < 2, got[:, 0], got[:, 1])
+    there = send(attention, CORE)
+    attention = jnp.where((core == 0) == (x < 2), attention, there)
+    spread = jnp.broadcast_to(attention[None], (8,) + attention.shape)
+    attention = lax.all_to_all(spread, ("yh", "z"), 0, 0, tiled=True)
     attention = attention.reshape(96, 1024)
     terms = jnp.dot(attention, o_weight, preferred_element_type=F32).reshape(32, STEPS, 512)
     terms = jnp.take(terms, slot_of, axis=0).reshape(8, 4, STEPS, 512)

time: 197 us -> 191 us (0.970)
  other arithmetic: 26 us -> 23 us
  Pallas kernels: 50.7 us -> 48.1 us
  local copies, waits for them, and re-layouts: 17.8 us -> 15.8 us
    ppermute x23 -> x24, waiting for transfers between devices: 26.7 us -> 30.6 us  [send(): return lax.ppermute(value, AXES, moves)]
    concatenate x10, other arithmetic: 15.4 us -> 12.6 us  [cat(): return jnp.concatenate(parts, axis=0)]
    pallas_call x1, Pallas kernels: 24.2 us -> 21.6 us  [project_keys(): pl.pallas_call(body, grid_spec=pltpu.PrefetchScalarGridSpec(num_scalar_pr...]
    all_to_all x1, waiting for transfers between devices: 10.9 us -> 8.34 us  [per_device(): attention = lax.all_to_all(spread, ('yh', 'z'), 0, 0, tiled=True)]
    ppermute x23 -> x24, starting transfers between devices: 34.5 us -> 35.7 us  [send(): return lax.ppermute(value, AXES, moves)]
    unnamed x49 -> x51, local copies, waits for them, and re-layouts: 5.99 us -> 5.16 us
  transfers between devices with their start and end apart: 24 -> 25, of which waited for: 8 -> 10; matrix products, arithmetic and copies ran while one was open for 17% -> 14% of each run, Pallas kernels for 26% -> 25%
where the time goes in v2:
time: 191 us; the launch traced here: 190 us
  Pallas kernels  48.1 us (25%)
  starting transfers between devices  40.4 us (21%)
  waiting for transfers between devices  39 us (20%)
  other arithmetic  23 us (12%)
  blocking collectives  19.7 us (10%)
  local copies, waits for them, and re-layouts  15.8 us (8%)
  matrix products  3.44 us (2%)
    ppermute x24, starting transfers between devices, send(): return lax.ppermute(value, AXES, moves)  35.7 us
    ppermute x24, waiting for transfers between devices, send(): return lax.ppermute(value, AXES, moves)  30.6 us
    pallas_call x2, Pallas kernels, project(): pl.pallas_call(body, grid_spec=pltpu.PrefetchScalarGridSpec(num_scalar_pr...  26.5 us
    pallas_call x1, Pallas kernels, project_keys(): pl.pallas_call(body, grid_spec=pltpu.PrefetchScalarGridSpec(num_scalar_pr...  21.6 us
    concatenate x10, other arithmetic, cat(): return jnp.concatenate(parts, axis=0)  12.6 us
    all_to_all x1, blocking collectives, per_device(): got = lax.all_to_all(cat(part, part), ('x', 'yl'), 0, 0, tiled=True)  10.5 us
    all_to_all x1, blocking collectives, per_device(): got = lax.all_to_all(terms, ('x', 'yl'), 0, 0, tiled=True)  9.2 us
    all_to_all x1, waiting for transfers between devices, per_device(): attention = lax.all_to_all(spread, ('yh', 'z'), 0, 0, tiled=True)  8.34 us
  transfers between devices with their start and end apart: 25, of which 10 were waited for; matrix products, arithmetic and copies ran while one was open for 14% of the time, Pallas kernels for 25%

profile of v2, /device:TPU:0, one launch (start us, length us, event | category | flops | bytes accessed | tf_op | source)
XLA Modules:
  0.0 190.3 jit_solution(8635065606891747509)
XLA Ops:
  0.0 1.6 constant_dynamic-slice_fusion
  9.0 1.7 dynamic-slice_select_fusion
  11.3 2.0 %collective-permute-start.3 = (bf16[512,256]{1,0:T(8,128)(2,1)S(1)}, bf16[512,256]{1,0:T(8,128)(2,1)S(1)}, u32[]{:S(2)}, u32[]{:S(2)}) collective-permute-start(bf16[512,256]{1,0:T(8,128)(2,1)S(1)} %get-tuple-element.64), channel_id=1, source_target_pairs={{0,16},{2,18},{4,20},{6,22},{8,56},{10,58},{12,60},{14,62},{16,0},... | collective-permute-start | bytes 786440 | tf_op jit(solution)/shard_map/ppermute | solution.py:63
  13.3 3.0 %collective-permute-start.2 = (bf16[256,512]{1,0:T(8,128)(2,1)}, bf16[256,512]{1,0:T(8,128)(2,1)S(1)}, u32[]{:S(2)}, u32[]{:S(2)}) collective-permute-start(bf16[256,512]{1,0:T(8,128)(2,1)} %dynamic-slice_select_fusion), channel_id=1, source_target_pairs={{0,65},{2,67},{4,69},{6,71},{8,73},{10,75},{12,77},{14,79},{16,81}... | collective-permute-start | bytes 786440 | tf_op jit(solution)/shard_map/ppermute | solution.py:63
  18.5 4.1 %collective-permute-start.5 = (bf16[1024,256]{1,0:T(8,128)(2,1)}, bf16[1024,256]{1,0:T(8,128)(2,1)}, u32[]{:S(2)}, u32[]{:S(2)}) collective-permute-start(bf16[1024,256]{1,0:T(8,128)(2,1)} %pad_maximum_fusion.7), channel_id=1, source_target_pairs={{0,48},{2,50},{4,52},{6,54},{8,24},{10,26},{12,28},{14,30},{16,32}... | collective-permute-start | bytes 1572872 | tf_op jit(solution)/shard_map/ppermute | solution.py:63
  22.7 3.0 %collective-permute-start.8 = (bf16[1024,256]{1,0:T(8,128)(2,1)}, bf16[1024,256]{1,0:T(8,128)(2,1)}, u32[]{:S(2)}, u32[]{:S(2)}) collective-permute-start(bf16[1024,256]{1,0:T(8,128)(2,1)} %pad_maximum_fusion.6), channel_id=1, source_target_pairs={{0,65},{2,67},{4,69},{6,71},{8,73},{10,75},{12,77},{14,79},{16,81}... | collective-permute-start | bytes 1572872 | tf_op jit(solution)/shard_map/ppermute | solution.py:63
  28.7 3.0 %collective-permute-done.5 = bf16[1024,256]{1,0:T(8,128)(2,1)} collective-permute-done((bf16[1024,256]{1,0:T(8,128)(2,1)}, bf16[1024,256]{1,0:T(8,128)(2,1)}, u32[]{:S(2)}, u32[]{:S(2)}) %collective-permute-start.5) | collective-permute-done | bytes 524320 | tf_op jit(solution)/shard_map/ppermute | solution.py:63
  31.6 2.2 %pad_maximum_fusion.3 = bf16[2048,256]{1,0:T(8,128)(2,1)} fusion(bf16[1024,256]{1,0:T(8,128)(2,1)} %collective-permute-done.5, bf16[512,256]{1,0:T(8,128)(2,1)} %copy-done.9, bf16[512,256]{1,0:T(8,128)(2,1)} %copy-done.7), kind=kLoop, calls=%fused_computation.16 | loop fusion | flops 3145728 | bytes 2097152 | tf_op jit(solution)/shard_map/concatenate | solution.py:67
  33.8 2.3 %collective-permute-done.4 = bf16[512,512]{1,0:T(8,128)(2,1)S(1)} collective-permute-done((bf16[512,512]{1,0:T(8,128)(2,1)S(1)}, bf16[512,512]{1,0:T(8,128)(2,1)S(1)}, u32[]{:S(2)}, u32[]{:S(2)}) %collective-permute-start.4) | collective-permute-done | bytes 524320 | tf_op jit(solution)/shard_map/ppermute | solution.py:63
  36.2 1.6 collective-permute-start.9
  40.3 2.1 %slice_add_fusion = f32[48,4096]{1,0:T(8,128)} fusion(f32[48,4096]{1,0:T(8,128)S(1)} %slice-done, f32[96,4096]{1,0:T(8,128)} %collective-permute-done.1), kind=kLoop, calls=%fused_computation.21 | loop fusion | flops 196608 | bytes 2359296 | tf_op jit(solution)/shard_map/add | solution.py:314
  42.9 5.5 %collective-permute-done.9.refs_13_ = bf16[768,512]{1,0:T(8,128)(2,1)} collective-permute-done((bf16[768,512]{1,0:T(8,128)(2,1)S(1)}, bf16[768,512]{1,0:T(8,128)(2,1)}, u32[]{:S(2)}, u32[]{:S(2)}) %collective-permute-start.9) | collective-permute-done | bytes 786464 | tf_op jit(solution)/shard_map/ppermute | solution.py:63
  49.4 2.1 %constant_dynamic-update-slice_fusion.2 = bf16[1536,512]{1,0:T(8,128)(2,1)} fusion(bf16[1536,512]{1,0:T(8,128)(2,1)} %copy-done.17, bf16[768,512]{1,0:T(8,128)(2,1)} %collective-permute-done.9.refs_13_), kind=kLoop, calls=%fused_computation.68 | loop fusion | bytes 1572864 | tf_op jit(solution)/shard_map/concatenate | solution.py:67
  51.5 2.8 %collective-permute-start.16 = (bf16[1536,512]{1,0:T(8,128)(2,1)}, bf16[1536,512]{1,0:T(8,128)(2,1)S(1)}, u32[]{:S(2)}, u32[]{:S(2)}) collective-permute-start(bf16[1536,512]{1,0:T(8,128)(2,1)} %constant_dynamic-update-slice_fusion.2), channel_id=1, source_target_pairs={{0,6},{2,4},{4,2},{6,0},{8,10},{10,8},{12,14},{14,12},{16,22},{18,... | collective-permute-start | bytes 4718600 | tf_op jit(solution)/shard_map/ppermute | solution.py:63
  55.5 8.6 %collective-permute-done.7.refs_8_ = bf16[1024,512]{1,0:T(8,128)(2,1)S(1)} collective-permute-done((bf16[1024,512]{1,0:T(8,128)(2,1)}, bf16[1024,512]{1,0:T(8,128)(2,1)S(1)}, u32[]{:S(2)}, u32[]{:S(2)}) %collective-permute-start.7) | collective-permute-done | bytes 1048608 | tf_op jit(solution)/shard_map/ppermute | solution.py:63
  66.5 2.9 %collective-permute-start.11 = (f32[24,4096]{1,0:T(8,128)S(1)}, f32[24,4096]{1,0:T(8,128)S(1)}, u32[]{:S(2)}, u32[]{:S(2)}) collective-permute-start(f32[24,4096]{1,0:T(8,128)S(1)} %slice.82), channel_id=1, source_target_pairs={{0,65},{2,67},{4,69},{6,71},{8,73},{10,75},{12,77},{14,79},{16,81}... | collective-permute-start | bytes 1179656 | tf_op jit(solution)/shard_map/ppermute | solution.py:63
  69.4 2.5 %pad_maximum_fusion.refs_4_.refs_8_ = bf16[4096,256]{1,0:T(8,128)(2,1)} fusion(bf16[2048,256]{1,0:T(8,128)(2,1)S(1)} %collective-permute-done.12, bf16[1024,256]{1,0:T(8,128)(2,1)} %collective-permute-done.5, bf16[512,256]{1,0:T(8,128)(2,1)S(1)} %copy-done.10, bf16[512,256]{1,0:T(8,128)(2,1)S(1)} %copy-done.8), kind=kLoop, calls=%fused_computation.3 | loop fusion | flops 8388608 | bytes 4194304 | tf_op jit(solution)/shard_map/concatenate | solution.py:67
  73.4 3.5 %collective-permute-done.11 = f32[24,4096]{1,0:T(8,128)S(1)} collective-permute-done((f32[24,4096]{1,0:T(8,128)S(1)}, f32[24,4096]{1,0:T(8,128)S(1)}, u32[]{:S(2)}, u32[]{:S(2)}) %collective-permute-start.11) | collective-permute-done | bytes 393248 | tf_op jit(solution)/shard_map/ppermute | solution.py:63
  77.0 3.0 %collective-permute-start.13 = (f32[12,4096]{1,0:T(8,128)S(1)}, f32[12,4096]{1,0:T(8,128)S(1)}, u32[]{:S(2)}, u32[]{:S(2)}) collective-permute-start(f32[12,4096]{1,0:T(8,128)S(1)} %slice.84), channel_id=1, source_target_pairs={{0,48},{2,50},{4,52},{6,54},{8,24},{10,26},{12,28},{14,30},{16,32}... | collective-permute-start | bytes 589832 | tf_op jit(solution)/shard_map/ppermute | solution.py:63
  80.0 2.5 %pad_maximum_fusion.1.refs_6_.refs_10_ = bf16[4096,256]{1,0:T(8,128)(2,1)} fusion(bf16[2048,256]{1,0:T(8,128)(2,1)S(1)} %collective-permute-done.14, bf16[1024,256]{1,0:T(8,128)(2,1)} %collective-permute-done.8, bf16[512,256]{1,0:T(8,128)(2,1)S(1)} %get-tuple-element.65, bf16[512,256]{1,0:T(8,128)(2,1)S(1)} %get-tuple-element.63), kind=kLoop, calls=%fused_computation.4 | loop fusion | flops 8388608 | bytes 4194304 | tf_op jit(solution)/shard_map/concatenate | solution.py:67
  82.8 1.8 collective-permute-done.13
  84.7 1.8 collective-permute-start.15
  87.7 12.9 %shard_map.91.refs_12_ = f32[2,800,512]{2,1,0:T(8,128)} custom-call(s32[16]{0:T(128)S(1)} %stack.567.idx_ref, bf16[800,8192]{1,0:T(8,128)(2,1)} %bitcast.221, bf16[800,8192]{1,0:T(8,128)(2,1)} %collective-permute-done.10.refs_1_.refs_3_.refs_5_.refs_7_, bf16[800,8192]{1,0:T(8,128)(2,1)} %bitcast.222, ...), custom_call_target="tpu_custom_call" | custom-call | flops 6710886400 | bytes 13107200 | tf_op jit(solution)/shard_map/pallas_call | solution.py:148
  102.8 2.9 %collective-permute-start.22 = (bf16[2048,512]{1,0:T(8,128)(2,1)}, bf16[2048,512]{1,0:T(8,128)(2,1)}, u32[]{:S(2)}, u32[]{:S(2)}) collective-permute-start(bf16[2048,512]{1,0:T(8,128)(2,1)} %constant_dynamic-update-slice_fusion.5), channel_id=1, source_target_pairs={{0,6},{2,4},{4,2},{6,0},{8,10},{10,8},{12,14},{14,12},{16,22},{18,... | collective-permute-start | bytes 6291464 | tf_op jit(solution)/shard_map/ppermute | solution.py:63
  106.7 3.4 %collective-permute-done.20.refs_7_.refs_11_ = bf16[4096,256]{1,0:T(8,128)(2,1)} collective-permute-done((bf16[4096,256]{1,0:T(8,128)(2,1)}, bf16[4096,256]{1,0:T(8,128)(2,1)}, u32[]{:S(2)}, u32[]{:S(2)}) %collective-permute-start.20) | collective-permute-done | bytes 2097184 | tf_op jit(solution)/shard_map/ppermute | solution.py:63
  110.1 21.6 %shard_map.92 = bf16[2,800,512]{2,1,0:T(8,128)(2,1)S(1)} custom-call(s32[48]{0:T(128)S(1)} %reshape.4440.idx_ref, bf16[800,8192]{1,0:T(8,128)(2,1)} %bitcast.225, bf16[800,8192]{1,0:T(8,128)(2,1)} %collective-permute-done.10.refs_1_.refs_3_.refs_5_.refs_7_, bf16[800,8192]{1,0:T(8,128)(2,1)} %bitcast.226, ...), custom_call_target="tpu_custom_call" | custom-call | flops 13421772800 | bytes 26214400 | tf_op jit(solution)/shard_map/pallas_call | solution.py:228
  131.7 3.5 %collective-permute-start.21 = (f32[12,4096]{1,0:T(8,128)S(1)}, f32[12,4096]{1,0:T(8,128)S(1)}, u32[]{:S(2)}, u32[]{:S(2)}) collective-permute-start(f32[12,4096]{1,0:T(8,128)S(1)} %add.811), channel_id=1, source_target_pairs={{0,6},{2,4},{4,2},{6,0},{8,10},{10,8},{12,14},{14,12},{16,22},{18,... | collective-permute-start | bytes 589832 | tf_op jit(solution)/shard_map/ppermute | solution.py:63
  135.2 13.6 %shard_map.93 = bf16[2,800,512]{2,1,0:T(8,128)(2,1)} custom-call(s32[16]{0:T(128)S(1)} %stack.641.idx_ref, bf16[800,8192]{1,0:T(8,128)(2,1)} %bitcast.227, bf16[800,8192]{1,0:T(8,128)(2,1)} %collective-permute-done.10.refs_1_.refs_3_.refs_5_.refs_7_, bf16[800,8192]{1,0:T(8,128)(2,1)} %bitcast.228, ...), custom_call_target="tpu_custom_call" | custom-call | flops 6710886400 | bytes 13107200 | tf_op jit(solution)/shard_map/pallas_call | solution.py:148
  152.9 10.5 %all_to_all.15 = bf16[8,2,96,128]{3,2,1,0:T(8,128)(2,1)S(1)} all-to-all(bf16[8,2,96,128]{3,2,1,0:T(8,128)(2,1)S(1)} %copy.71), channel_id=1, replica_groups=mesh['yh'=2,'z'=4,'c'=2,'x'=4,'yl'=2] {'x','yl'}, dimensions={0} | all-to-all | bytes 786432 | tf_op jit(solution)/shard_map/all_to_all | solution.py:406
  165.9 4.7 %all-to-all-start.1 = ((bf16[8,2,48,128]{3,2,1,0:T(8,128)(2,1)}), bf16[8,2,48,128]{3,2,1,0:T(8,128)(2,1)S(1)}, u32[]{:S(2)}, u32[]{:S(2)}) async-start(bf16[8,2,48,128]{3,2,1,0:T(8,128)(2,1)} %broadcast_in_dim.86), calls=%async_computation.1 | async-start | bytes 393216 | tf_op jit(solution)/shard_map/all_to_all | solution.py:415
  170.7 8.3 %all-to-all-done.1 = bf16[8,2,48,128]{3,2,1,0:T(8,128)(2,1)S(1)} async-done(((bf16[8,2,48,128]{3,2,1,0:T(8,128)(2,1)}), bf16[8,2,48,128]{3,2,1,0:T(8,128)(2,1)S(1)}, u32[]{:S(2)}, u32[]{:S(2)}) %all-to-all-start.1) | async-done | bytes 196640 | tf_op jit(solution)/shard_map/all_to_all | solution.py:415
  180.4 9.2 %all_to_all.16 = f32[8,4,3,512]{3,1,2,0:T(4,128)S(1)} all-to-all(f32[8,4,3,512]{3,1,2,0:T(4,128)S(1)} %copy_select_fusion), channel_id=1, replica_groups=mesh['yh'=2,'z'=4,'c'=2,'x'=4,'yl'=2] {'x','yl'}, dimensions={0} | all-to-all | bytes 393216 | tf_op jit(solution)/shard_map/all_to_all | solution.py:419
  (167 shorter events, 35.1 us)
Async XLA Ops:
  1.7 4.3 %collective-permute-start = (bf16[1024,512]{1,0:T(8,128)(2,1)S(1)}, bf16[1024,512]{1,0:T(8,128)(2,1)}, u32[]{:S(2)}, u32[]{:S(2)}) collective-permute-start(bf16[1024,512]{1,0:T(8,128)(2,1)S(1)} %pad_maximum_fusion.2), channel_id=1, source_target_pairs={{0,8},{2,10},{4,12},{6,14},{8,0},{10,2},{12,4},{14,6},{16,24},{18,... | collective-permute-start | bytes 3145736 | tf_op jit(solution)/shard_map/ppermute | solution.py:63
  8.2 19.2 %copy-start.7 = (bf16[512,256]{1,0:T(8,128)(2,1)}, bf16[512,256]{1,0:T(8,128)(2,1)S(1)}, u32[]{:S(2)}) copy-start(bf16[512,256]{1,0:T(8,128)(2,1)S(1)} %get-tuple-element.64) | copy-start | bytes 786436
  10.7 38.7 %collective-permute-start.10 = (bf16[800,8192]{1,0:T(8,128)(2,1)}, bf16[800,8192]{1,0:T(8,128)(2,1)}, u32[]{:S(2)}, u32[]{:S(2)}) collective-permute-start(bf16[800,8192]{1,0:T(8,128)(2,1)} %bitcast.220), channel_id=1, source_target_pairs={{0,8},{2,10},{4,12},{6,14},{8,0},{10,2},{12,4},{14,6},{16,24},{18,... | collective-permute-start | bytes 39321608 | tf_op jit(solution)/shard_map/ppermute | solution.py:63
  11.2 29.1 %collective-permute-start.1 = (f32[96,4096]{1,0:T(8,128)}, f32[96,4096]{1,0:T(8,128)}, u32[]{:S(2)}, u32[]{:S(2)}) collective-permute-start(f32[96,4096]{1,0:T(8,128)} %fusion.20), channel_id=1, source_target_pairs={{0,8},{2,10},{4,12},{6,14},{8,0},{10,2},{12,4},{14,6},{16,24},{18,... | collective-permute-start | bytes 4718600 | tf_op jit(solution)/shard_map/ppermute | solution.py:63
  11.3 6.4 %collective-permute-start.3 = (bf16[512,256]{1,0:T(8,128)(2,1)S(1)}, bf16[512,256]{1,0:T(8,128)(2,1)S(1)}, u32[]{:S(2)}, u32[]{:S(2)}) collective-permute-start(bf16[512,256]{1,0:T(8,128)(2,1)S(1)} %get-tuple-element.64), channel_id=1, source_target_pairs={{0,16},{2,18},{4,20},{6,22},{8,56},{10,58},{12,60},{14,62},{16,0},... | collective-permute-start | bytes 786440 | tf_op jit(solution)/shard_map/ppermute | solution.py:63
  13.3 12.5 %collective-permute-start.2 = (bf16[256,512]{1,0:T(8,128)(2,1)}, bf16[256,512]{1,0:T(8,128)(2,1)S(1)}, u32[]{:S(2)}, u32[]{:S(2)}) collective-permute-start(bf16[256,512]{1,0:T(8,128)(2,1)} %dynamic-slice_select_fusion), channel_id=1, source_target_pairs={{0,65},{2,67},{4,69},{6,71},{8,73},{10,75},{12,77},{14,79},{16,81}... | collective-permute-start | bytes 786440 | tf_op jit(solution)/shard_map/ppermute | solution.py:63
  18.5 13.1 %collective-permute-start.5 = (bf16[1024,256]{1,0:T(8,128)(2,1)}, bf16[1024,256]{1,0:T(8,128)(2,1)}, u32[]{:S(2)}, u32[]{:S(2)}) collective-permute-start(bf16[1024,256]{1,0:T(8,128)(2,1)} %pad_maximum_fusion.7), channel_id=1, source_target_pairs={{0,48},{2,50},{4,52},{6,54},{8,24},{10,26},{12,28},{14,30},{16,32}... | collective-permute-start | bytes 1572872 | tf_op jit(solution)/shard_map/ppermute | solution.py:63
  22.7 31.5 %collective-permute-start.8 = (bf16[1024,256]{1,0:T(8,128)(2,1)}, bf16[1024,256]{1,0:T(8,128)(2,1)}, u32[]{:S(2)}, u32[]{:S(2)}) collective-permute-start(bf16[1024,256]{1,0:T(8,128)(2,1)} %pad_maximum_fusion.6), channel_id=1, source_target_pairs={{0,65},{2,67},{4,69},{6,71},{8,73},{10,75},{12,77},{14,79},{16,81}... | collective-permute-start | bytes 1572872 | tf_op jit(solution)/shard_map/ppermute | solution.py:63
  26.9 9.3 %collective-permute-start.4 = (bf16[512,512]{1,0:T(8,128)(2,1)S(1)}, bf16[512,512]{1,0:T(8,128)(2,1)S(1)}, u32[]{:S(2)}, u32[]{:S(2)}) collective-permute-start(bf16[512,512]{1,0:T(8,128)(2,1)S(1)} %pad_maximum_fusion.8), channel_id=1, source_target_pairs={{0,16},{2,18},{4,20},{6,22},{8,56},{10,58},{12,60},{14,62},{16,0},... | collective-permute-start | bytes 1572872 | tf_op jit(solution)/shard_map/ppermute | solution.py:63
  27.4 10.4 %copy-start.12 = (bf16[256,512]{1,0:T(8,128)(2,1)S(1)}, bf16[256,512]{1,0:T(8,128)(2,1)}, u32[]{:S(2)}) copy-start(bf16[256,512]{1,0:T(8,128)(2,1)} %copy-done.11) | copy-start | bytes 786436
  36.2 12.2 %collective-permute-start.9 = (bf16[768,512]{1,0:T(8,128)(2,1)S(1)}, bf16[768,512]{1,0:T(8,128)(2,1)}, u32[]{:S(2)}, u32[]{:S(2)}) collective-permute-start(bf16[768,512]{1,0:T(8,128)(2,1)S(1)} %get-tuple-element.67.refs_12_), channel_id=1, source_target_pairs={{0,2},{2,0},{4,6},{6,4},{8,14},{10,12},{12,10},{14,8},{16,18},{18,... | collective-permute-start | bytes 2359304 | tf_op jit(solution)/shard_map/ppermute | solution.py:63
  38.9 25.2 %collective-permute-start.7 = (bf16[1024,512]{1,0:T(8,128)(2,1)}, bf16[1024,512]{1,0:T(8,128)(2,1)S(1)}, u32[]{:S(2)}, u32[]{:S(2)}) collective-permute-start(bf16[1024,512]{1,0:T(8,128)(2,1)} %pad_maximum_fusion.4), channel_id=1, source_target_pairs={{0,48},{2,50},{4,52},{6,54},{8,24},{10,26},{12,28},{14,30},{16,32}... | collective-permute-start | bytes 3145736 | tf_op jit(solution)/shard_map/ppermute | solution.py:63
  42.4 22.5 %collective-permute-start.6 = (f32[48,4096]{1,0:T(8,128)}, f32[48,4096]{1,0:T(8,128)}, u32[]{:S(2)}, u32[]{:S(2)}) collective-permute-start(f32[48,4096]{1,0:T(8,128)} %slice_add_fusion), channel_id=1, source_target_pairs={{0,16},{2,18},{4,20},{6,22},{8,56},{10,58},{12,60},{14,62},{16,0},... | collective-permute-start | bytes 2359304 | tf_op jit(solution)/shard_map/ppermute | solution.py:63
  42.7 22.3 %copy-start.4 = (f32[96,4096]{1,0:T(8,128)S(1)}, f32[96,4096]{1,0:T(8,128)}, u32[]{:S(2)}) copy-start(f32[96,4096]{1,0:T(8,128)} %copy-done.3) | copy-start | bytes 4718596
  48.4 18.1 %collective-permute-start.12 = (bf16[2048,256]{1,0:T(8,128)(2,1)}, bf16[2048,256]{1,0:T(8,128)(2,1)S(1)}, u32[]{:S(2)}, u32[]{:S(2)}) collective-permute-start(bf16[2048,256]{1,0:T(8,128)(2,1)} %pad_maximum_fusion.3), channel_id=1, source_target_pairs={{0,1},{2,3},{4,5},{6,7},{8,73},{10,75},{12,77},{14,79},{16,17},{18... | collective-permute-start | bytes 3145736 | tf_op jit(solution)/shard_map/ppermute | solution.py:63
  51.5 35.0 %collective-permute-start.16 = (bf16[1536,512]{1,0:T(8,128)(2,1)}, bf16[1536,512]{1,0:T(8,128)(2,1)S(1)}, u32[]{:S(2)}, u32[]{:S(2)}) collective-permute-start(bf16[1536,512]{1,0:T(8,128)(2,1)} %constant_dynamic-update-slice_fusion.2), channel_id=1, source_target_pairs={{0,6},{2,4},{4,2},{6,0},{8,10},{10,8},{12,14},{14,12},{16,22},{18,... | collective-permute-start | bytes 4718600 | tf_op jit(solution)/shard_map/ppermute | solution.py:63
  55.4 14.0 %copy-start.8 = (bf16[512,256]{1,0:T(8,128)(2,1)S(1)}, bf16[512,256]{1,0:T(8,128)(2,1)}, u32[]{:S(2)}) copy-start(bf16[512,256]{1,0:T(8,128)(2,1)} %copy-done.7) | copy-start | bytes 786436
  55.4 14.0 %copy-start.10 = (bf16[512,256]{1,0:T(8,128)(2,1)S(1)}, bf16[512,256]{1,0:T(8,128)(2,1)}, u32[]{:S(2)}) copy-start(bf16[512,256]{1,0:T(8,128)(2,1)} %copy-done.9) | copy-start | bytes 786436
  55.4 24.6 %collective-permute-start.14 = (bf16[2048,256]{1,0:T(8,128)(2,1)S(1)}, bf16[2048,256]{1,0:T(8,128)(2,1)S(1)}, u32[]{:S(2)}, u32[]{:S(2)}) collective-permute-start(bf16[2048,256]{1,0:T(8,128)(2,1)S(1)} %pad_maximum_fusion.5), channel_id=1, source_target_pairs={{0,16},{2,18},{4,20},{6,22},{8,56},{10,58},{12,60},{14,62},{16,0},... | collective-permute-start | bytes 3145736 | tf_op jit(solution)/shard_map/ppermute | solution.py:63
  64.1 36.6 %collective-permute-start.19 = (bf16[1024,512]{1,0:T(8,128)(2,1)S(1)}, bf16[1024,512]{1,0:T(8,128)(2,1)S(1)}, u32[]{:S(2)}, u32[]{:S(2)}) collective-permute-start(bf16[1024,512]{1,0:T(8,128)(2,1)S(1)} %collective-permute-done.7.refs_8_), channel_id=1, source_target_pairs={{0,2},{2,0},{4,6},{6,4},{8,14},{10,12},{12,10},{14,8},{16,18},{18,... | collective-permute-start | bytes 3145736 | tf_op jit(solution)/shard_map/ppermute | solution.py:63
  66.5 10.4 %collective-permute-start.11 = (f32[24,4096]{1,0:T(8,128)S(1)}, f32[24,4096]{1,0:T(8,128)S(1)}, u32[]{:S(2)}, u32[]{:S(2)}) collective-permute-start(f32[24,4096]{1,0:T(8,128)S(1)} %slice.82), channel_id=1, source_target_pairs={{0,65},{2,67},{4,69},{6,71},{8,73},{10,75},{12,77},{14,79},{16,81}... | collective-permute-start | bytes 1179656 | tf_op jit(solution)/shard_map/ppermute | solution.py:63
  71.9 34.8 %collective-permute-start.18 = (bf16[4096,256]{1,0:T(8,128)(2,1)}, bf16[4096,256]{1,0:T(8,128)(2,1)}, u32[]{:S(2)}, u32[]{:S(2)}) collective-permute-start(bf16[4096,256]{1,0:T(8,128)(2,1)} %pad_maximum_fusion.refs_4_.refs_8_), channel_id=1, source_target_pairs={{0,65},{2,67},{4,69},{6,71},{8,9},{10,11},{12,13},{14,15},{16,81},... | collective-permute-start | bytes 6291464 | tf_op jit(solution)/shard_map/ppermute | solution.py:63
  77.0 7.7 %collective-permute-start.13 = (f32[12,4096]{1,0:T(8,128)S(1)}, f32[12,4096]{1,0:T(8,128)S(1)}, u32[]{:S(2)}, u32[]{:S(2)}) collective-permute-start(f32[12,4096]{1,0:T(8,128)S(1)} %slice.84), channel_id=1, source_target_pairs={{0,48},{2,50},{4,52},{6,54},{8,24},{10,26},{12,28},{14,30},{16,32}... | collective-permute-start | bytes 589832 | tf_op jit(solution)/shard_map/ppermute | solution.py:63
  82.5 27.6 %collective-permute-start.20 = (bf16[4096,256]{1,0:T(8,128)(2,1)}, bf16[4096,256]{1,0:T(8,128)(2,1)}, u32[]{:S(2)}, u32[]{:S(2)}) collective-permute-start(bf16[4096,256]{1,0:T(8,128)(2,1)} %pad_maximum_fusion.1.refs_6_.refs_10_), channel_id=1, source_target_pairs={{0,48},{2,50},{4,52},{6,54},{8,24},{10,26},{12,28},{14,30},{16,32}... | collective-permute-start | bytes 6291464 | tf_op jit(solution)/shard_map/ppermute | solution.py:63
  84.7 16.0 %collective-permute-start.15 = (f32[12,4096]{1,0:T(8,128)S(1)}, f32[12,4096]{1,0:T(8,128)S(1)}, u32[]{:S(2)}, u32[]{:S(2)}) collective-permute-start(f32[12,4096]{1,0:T(8,128)S(1)} %slice_add_fusion.3), channel_id=1, source_target_pairs={{0,1},{2,3},{4,5},{6,7},{8,9},{10,11},{12,13},{14,15},{16,17},{18,... | collective-permute-start | bytes 589832 | tf_op jit(solution)/shard_map/ppermute | solution.py:63
  102.8 32.4 %collective-permute-start.22 = (bf16[2048,512]{1,0:T(8,128)(2,1)}, bf16[2048,512]{1,0:T(8,128)(2,1)}, u32[]{:S(2)}, u32[]{:S(2)}) collective-permute-start(bf16[2048,512]{1,0:T(8,128)(2,1)} %constant_dynamic-update-slice_fusion.5), channel_id=1, source_target_pairs={{0,6},{2,4},{4,2},{6,0},{8,10},{10,8},{12,14},{14,12},{16,22},{18,... | collective-permute-start | bytes 6291464 | tf_op jit(solution)/shard_map/ppermute | solution.py:63
  106.5 25.2 %collective-permute-start.17 = (f32[12,4096]{1,0:T(8,128)S(1)}, f32[12,4096]{1,0:T(8,128)S(1)}, u32[]{:S(2)}, u32[]{:S(2)}) collective-permute-start(f32[12,4096]{1,0:T(8,128)S(1)} %add.755), channel_id=1, source_target_pairs={{0,2},{2,0},{4,6},{6,4},{8,14},{10,12},{12,10},{14,8},{16,18},{18,... | collective-permute-start | bytes 589832 | tf_op jit(solution)/shard_map/ppermute | solution.py:63
  131.7 17.2 %collective-permute-start.21 = (f32[12,4096]{1,0:T(8,128)S(1)}, f32[12,4096]{1,0:T(8,128)S(1)}, u32[]{:S(2)}, u32[]{:S(2)}) collective-permute-start(f32[12,4096]{1,0:T(8,128)S(1)} %add.811), channel_id=1, source_target_pairs={{0,6},{2,4},{4,2},{6,0},{8,10},{10,8},{12,14},{14,12},{16,22},{18,... | collective-permute-start | bytes 589832 | tf_op jit(solution)/shard_map/ppermute | solution.py:63
  152.9 26.2 %copy-start.15 = (bf16[1024,512]{1,0:T(8,128)(2,1)S(1)}, bf16[1024,512]{1,0:T(8,128)(2,1)}, u32[]{:S(2)}) copy-start(bf16[1024,512]{1,0:T(8,128)(2,1)} %param.17) | copy-start | bytes 3145732
  164.0 1.3 collective-permute-start.23
  165.2 25.0 %copy-start.1 = (bf16[64,8192]{1,0:T(8,128)(2,1)S(1)}, bf16[64,8192]{1,0:T(8,128)(2,1)}, u32[]{:S(2)}) copy-start(bf16[64,8192]{1,0:T(8,128)(2,1)} %param.13) | copy-start | bytes 3145732
  165.9 13.1 %all-to-all-start.1 = ((bf16[8,2,48,128]{3,2,1,0:T(8,128)(2,1)}), bf16[8,2,48,128]{3,2,1,0:T(8,128)(2,1)S(1)}, u32[]{:S(2)}, u32[]{:S(2)}) async-start(bf16[8,2,48,128]{3,2,1,0:T(8,128)(2,1)} %broadcast_in_dim.86), calls=%async_computation.1 | async-start | bytes 393216 | tf_op jit(solution)/shard_map/all_to_all | solution.py:415
  (15 other events, 63.9 us)

commit v3 on v2

--- a/solution.py
+++ b/solution.py
@@ -397,15 +397,15 @@
     high = lax.reduce_precision(weight, 8, 7)
     middle = lax.reduce_precision(weight - high, 8, 7)
     low = lax.reduce_precision(weight - high - middle, 8, 7)
-    weight = jnp.stack([high, middle, low], axis=-1)
-    weight = jnp.pad(weight, ((0, 0),) * 3 + ((0, HD - 3),))
+    weight = jnp.stack([high, middle, low], axis=2)
+    weight = jnp.pad(weight, ((0, 0), (0, 0), (0, 13), (0, HD - 48)))
     value_heads = value_heads.reshape(2, 800, 4, HD)
     part = jnp.einsum("ikrt,itkd->ikrd", probs, value_heads, preferred_element_type=F32)
     part = jnp.concatenate([part, weight], axis=2).astype(BF16)
     part = jnp.where(core == 0, part, part[::-1]).transpose(1, 0, 2, 3)
     got = lax.all_to_all(cat(part, part), ("x", "yl"), 0, 0, tiled=True)
     got = got.astype(F32)
-    weight = jnp.sum(got[:, :, 48:, :3], axis=-1, keepdims=True)
+    weight = jnp.sum(got[:, :, 48:51, :48], axis=2)[..., None]
     weight = jnp.exp(weight - jnp.max(weight, axis=0, keepdims=True))
     weight = weight / jnp.sum(weight, axis=0, keepdims=True)
     attention = jnp.sum(got[:, :, :48] * weight, axis=0).astype(BF16)

time: 191 us -> 189 us (0.990)
    unnamed x51 -> x52, local copies, waits for them, and re-layouts: 5.16 us -> 5.16 us
  transfers between devices with their start and end apart: 25 -> 25, of which waited for: 10 -> 10; matrix products, arithmetic and copies ran while one was open for 14% -> 14% of each run, Pallas kernels for 25% -> 26%
where the time goes in v3:
time: 189 us; the launch traced here: 188 us
  Pallas kernels  48.1 us (25%)
  starting transfers between devices  40.4 us (21%)
  waiting for transfers between devices  39 us (21%)
  other arithmetic  22 us (12%)
  blocking collectives  18.9 us (10%)
  local copies, waits for them, and re-layouts  15.3 us (8%)
  matrix products  3.44 us (2%)
    ppermute x24, starting transfers between devices, send(): return lax.ppermute(value, AXES, moves)  35.7 us
    ppermute x24, waiting for transfers between devices, send(): return lax.ppermute(value, AXES, moves)  30.6 us
    pallas_call x2, Pallas kernels, project(): pl.pallas_call(body, grid_spec=pltpu.PrefetchScalarGridSpec(num_scalar_pr...  26.5 us
    pallas_call x1, Pallas kernels, project_keys(): pl.pallas_call(body, grid_spec=pltpu.PrefetchScalarGridSpec(num_scalar_pr...  21.6 us
    concatenate x10, other arithmetic, cat(): return jnp.concatenate(parts, axis=0)  12.3 us
    all_to_all x1, blocking collectives, per_device(): got = lax.all_to_all(cat(part, part), ('x', 'yl'), 0, 0, tiled=True)  9.65 us
    all_to_all x1, blocking collectives, per_device(): got = lax.all_to_all(terms, ('x', 'yl'), 0, 0, tiled=True)  9.2 us
    all_to_all x1, waiting for transfers between devices, per_device(): attention = lax.all_to_all(spread, ('yh', 'z'), 0, 0, tiled=True)  8.34 us
  transfers between devices with their start and end apart: 25, of which 10 were waited for; matrix products, arithmetic and copies ran while one was open for 14% of the time, Pallas kernels for 26%

profile of v3, /device:TPU:0, one launch (start us, length us, event | category | flops | bytes accessed | tf_op | source)
XLA Modules:
  0.0 187.9 jit_solution(15000424107668833629)
XLA Ops:
  0.0 1.6 constant_dynamic-slice_fusion
  9.0 1.7 dynamic-slice_select_fusion
  11.3 2.0 %collective-permute-start.3 = (bf16[512,256]{1,0:T(8,128)(2,1)S(1)}, bf16[512,256]{1,0:T(8,128)(2,1)S(1)}, u32[]{:S(2)}, u32[]{:S(2)}) collective-permute-start(bf16[512,256]{1,0:T(8,128)(2,1)S(1)} %get-tuple-element.64), channel_id=1, source_target_pairs={{0,16},{2,18},{4,20},{6,22},{8,56},{10,58},{12,60},{14,62},{16,0},... | collective-permute-start | bytes 786440 | tf_op jit(solution)/shard_map/ppermute | solution.py:63
  13.3 3.0 %collective-permute-start.2 = (bf16[256,512]{1,0:T(8,128)(2,1)}, bf16[256,512]{1,0:T(8,128)(2,1)S(1)}, u32[]{:S(2)}, u32[]{:S(2)}) collective-permute-start(bf16[256,512]{1,0:T(8,128)(2,1)} %dynamic-slice_select_fusion), channel_id=1, source_target_pairs={{0,65},{2,67},{4,69},{6,71},{8,73},{10,75},{12,77},{14,79},{16,81}... | collective-permute-start | bytes 786440 | tf_op jit(solution)/shard_map/ppermute | solution.py:63
  18.5 4.1 %collective-permute-start.5 = (bf16[1024,256]{1,0:T(8,128)(2,1)}, bf16[1024,256]{1,0:T(8,128)(2,1)}, u32[]{:S(2)}, u32[]{:S(2)}) collective-permute-start(bf16[1024,256]{1,0:T(8,128)(2,1)} %pad_maximum_fusion.7), channel_id=1, source_target_pairs={{0,48},{2,50},{4,52},{6,54},{8,24},{10,26},{12,28},{14,30},{16,32}... | collective-permute-start | bytes 1572872 | tf_op jit(solution)/shard_map/ppermute | solution.py:63
  22.7 3.0 %collective-permute-start.8 = (bf16[1024,256]{1,0:T(8,128)(2,1)}, bf16[1024,256]{1,0:T(8,128)(2,1)}, u32[]{:S(2)}, u32[]{:S(2)}) collective-permute-start(bf16[1024,256]{1,0:T(8,128)(2,1)} %pad_maximum_fusion.6), channel_id=1, source_target_pairs={{0,65},{2,67},{4,69},{6,71},{8,73},{10,75},{12,77},{14,79},{16,81}... | collective-permute-start | bytes 1572872 | tf_op jit(solution)/shard_map/ppermute | solution.py:63
  28.7 3.0 %collective-permute-done.5 = bf16[1024,256]{1,0:T(8,128)(2,1)} collective-permute-done((bf16[1024,256]{1,0:T(8,128)(2,1)}, bf16[1024,256]{1,0:T(8,128)(2,1)}, u32[]{:S(2)}, u32[]{:S(2)}) %collective-permute-start.5) | collective-permute-done | bytes 524320 | tf_op jit(solution)/shard_map/ppermute | solution.py:63
  31.6 2.2 %pad_maximum_fusion.3 = bf16[2048,256]{1,0:T(8,128)(2,1)} fusion(bf16[1024,256]{1,0:T(8,128)(2,1)} %collective-permute-done.5, bf16[512,256]{1,0:T(8,128)(2,1)} %copy-done.9, bf16[512,256]{1,0:T(8,128)(2,1)} %copy-done.7), kind=kLoop, calls=%fused_computation.17 | loop fusion | flops 3145728 | bytes 2097152 | tf_op jit(solution)/shard_map/concatenate | solution.py:67
  33.8 2.3 %collective-permute-done.4 = bf16[512,512]{1,0:T(8,128)(2,1)S(1)} collective-permute-done((bf16[512,512]{1,0:T(8,128)(2,1)S(1)}, bf16[512,512]{1,0:T(8,128)(2,1)S(1)}, u32[]{:S(2)}, u32[]{:S(2)}) %collective-permute-start.4) | collective-permute-done | bytes 524320 | tf_op jit(solution)/shard_map/ppermute | solution.py:63
  36.2 1.6 collective-permute-start.9
  40.3 2.1 %slice_add_fusion = f32[48,4096]{1,0:T(8,128)} fusion(f32[48,4096]{1,0:T(8,128)S(1)} %slice-done, f32[96,4096]{1,0:T(8,128)} %collective-permute-done.1), kind=kLoop, calls=%fused_computation.22 | loop fusion | flops 196608 | bytes 2359296 | tf_op jit(solution)/shard_map/add | solution.py:314
  42.9 5.5 %collective-permute-done.9.refs_13_ = bf16[768,512]{1,0:T(8,128)(2,1)} collective-permute-done((bf16[768,512]{1,0:T(8,128)(2,1)S(1)}, bf16[768,512]{1,0:T(8,128)(2,1)}, u32[]{:S(2)}, u32[]{:S(2)}) %collective-permute-start.9) | collective-permute-done | bytes 786464 | tf_op jit(solution)/shard_map/ppermute | solution.py:63
  49.4 2.1 %constant_dynamic-update-slice_fusion.2 = bf16[1536,512]{1,0:T(8,128)(2,1)} fusion(bf16[1536,512]{1,0:T(8,128)(2,1)} %copy-done.17, bf16[768,512]{1,0:T(8,128)(2,1)} %collective-permute-done.9.refs_13_), kind=kLoop, calls=%fused_computation.65 | loop fusion | bytes 1572864 | tf_op jit(solution)/shard_map/concatenate | solution.py:67
  51.5 2.8 %collective-permute-start.16 = (bf16[1536,512]{1,0:T(8,128)(2,1)}, bf16[1536,512]{1,0:T(8,128)(2,1)S(1)}, u32[]{:S(2)}, u32[]{:S(2)}) collective-permute-start(bf16[1536,512]{1,0:T(8,128)(2,1)} %constant_dynamic-update-slice_fusion.2), channel_id=1, source_target_pairs={{0,6},{2,4},{4,2},{6,0},{8,10},{10,8},{12,14},{14,12},{16,22},{18,... | collective-permute-start | bytes 4718600 | tf_op jit(solution)/shard_map/ppermute | solution.py:63
  55.5 8.6 %collective-permute-done.7.refs_8_ = bf16[1024,512]{1,0:T(8,128)(2,1)S(1)} collective-permute-done((bf16[1024,512]{1,0:T(8,128)(2,1)}, bf16[1024,512]{1,0:T(8,128)(2,1)S(1)}, u32[]{:S(2)}, u32[]{:S(2)}) %collective-permute-start.7) | collective-permute-done | bytes 1048608 | tf_op jit(solution)/shard_map/ppermute | solution.py:63
  66.5 2.9 %collective-permute-start.11 = (f32[24,4096]{1,0:T(8,128)S(1)}, f32[24,4096]{1,0:T(8,128)S(1)}, u32[]{:S(2)}, u32[]{:S(2)}) collective-permute-start(f32[24,4096]{1,0:T(8,128)S(1)} %slice.82), channel_id=1, source_target_pairs={{0,65},{2,67},{4,69},{6,71},{8,73},{10,75},{12,77},{14,79},{16,81}... | collective-permute-start | bytes 1179656 | tf_op jit(solution)/shard_map/ppermute | solution.py:63
  69.4 2.5 %pad_maximum_fusion.refs_4_.refs_8_ = bf16[4096,256]{1,0:T(8,128)(2,1)} fusion(bf16[2048,256]{1,0:T(8,128)(2,1)S(1)} %collective-permute-done.12, bf16[1024,256]{1,0:T(8,128)(2,1)} %collective-permute-done.5, bf16[512,256]{1,0:T(8,128)(2,1)S(1)} %copy-done.10, bf16[512,256]{1,0:T(8,128)(2,1)S(1)} %copy-done.8), kind=kLoop, calls=%fused_computation.3 | loop fusion | flops 8388608 | bytes 4194304 | tf_op jit(solution)/shard_map/concatenate | solution.py:67
  73.4 3.5 %collective-permute-done.11 = f32[24,4096]{1,0:T(8,128)S(1)} collective-permute-done((f32[24,4096]{1,0:T(8,128)S(1)}, f32[24,4096]{1,0:T(8,128)S(1)}, u32[]{:S(2)}, u32[]{:S(2)}) %collective-permute-start.11) | collective-permute-done | bytes 393248 | tf_op jit(solution)/shard_map/ppermute | solution.py:63
  77.0 3.0 %collective-permute-start.13 = (f32[12,4096]{1,0:T(8,128)S(1)}, f32[12,4096]{1,0:T(8,128)S(1)}, u32[]{:S(2)}, u32[]{:S(2)}) collective-permute-start(f32[12,4096]{1,0:T(8,128)S(1)} %slice.84), channel_id=1, source_target_pairs={{0,48},{2,50},{4,52},{6,54},{8,24},{10,26},{12,28},{14,30},{16,32}... | collective-permute-start | bytes 589832 | tf_op jit(solution)/shard_map/ppermute | solution.py:63
  80.0 2.5 %pad_maximum_fusion.1.refs_6_.refs_10_ = bf16[4096,256]{1,0:T(8,128)(2,1)} fusion(bf16[2048,256]{1,0:T(8,128)(2,1)S(1)} %collective-permute-done.14, bf16[1024,256]{1,0:T(8,128)(2,1)} %collective-permute-done.8, bf16[512,256]{1,0:T(8,128)(2,1)S(1)} %get-tuple-element.65, bf16[512,256]{1,0:T(8,128)(2,1)S(1)} %get-tuple-element.63), kind=kLoop, calls=%fused_computation.4 | loop fusion | flops 8388608 | bytes 4194304 | tf_op jit(solution)/shard_map/concatenate | solution.py:67
  82.8 1.8 collective-permute-done.13
  84.7 1.8 collective-permute-start.15
  87.7 12.9 %shard_map.91.refs_12_ = f32[2,800,512]{2,1,0:T(8,128)} custom-call(s32[16]{0:T(128)S(1)} %stack.567.idx_ref, bf16[800,8192]{1,0:T(8,128)(2,1)} %bitcast.220, bf16[800,8192]{1,0:T(8,128)(2,1)} %collective-permute-done.10.refs_1_.refs_3_.refs_5_.refs_7_, bf16[800,8192]{1,0:T(8,128)(2,1)} %bitcast.221, ...), custom_call_target="tpu_custom_call" | custom-call | flops 6710886400 | bytes 13107200 | tf_op jit(solution)/shard_map/pallas_call | solution.py:148
  102.8 2.9 %collective-permute-start.22 = (bf16[2048,512]{1,0:T(8,128)(2,1)}, bf16[2048,512]{1,0:T(8,128)(2,1)}, u32[]{:S(2)}, u32[]{:S(2)}) collective-permute-start(bf16[2048,512]{1,0:T(8,128)(2,1)} %constant_dynamic-update-slice_fusion.5), channel_id=1, source_target_pairs={{0,6},{2,4},{4,2},{6,0},{8,10},{10,8},{12,14},{14,12},{16,22},{18,... | collective-permute-start | bytes 6291464 | tf_op jit(solution)/shard_map/ppermute | solution.py:63
  106.7 3.4 %collective-permute-done.20.refs_7_.refs_11_ = bf16[4096,256]{1,0:T(8,128)(2,1)} collective-permute-done((bf16[4096,256]{1,0:T(8,128)(2,1)}, bf16[4096,256]{1,0:T(8,128)(2,1)}, u32[]{:S(2)}, u32[]{:S(2)}) %collective-permute-start.20) | collective-permute-done | bytes 2097184 | tf_op jit(solution)/shard_map/ppermute | solution.py:63
  110.1 21.6 %shard_map.92 = bf16[2,800,512]{2,1,0:T(8,128)(2,1)S(1)} custom-call(s32[48]{0:T(128)S(1)} %reshape.4440.idx_ref, bf16[800,8192]{1,0:T(8,128)(2,1)} %bitcast.224, bf16[800,8192]{1,0:T(8,128)(2,1)} %collective-permute-done.10.refs_1_.refs_3_.refs_5_.refs_7_, bf16[800,8192]{1,0:T(8,128)(2,1)} %bitcast.225, ...), custom_call_target="tpu_custom_call" | custom-call | flops 13421772800 | bytes 26214400 | tf_op jit(solution)/shard_map/pallas_call | solution.py:228
  131.7 3.5 %collective-permute-start.21 = (f32[12,4096]{1,0:T(8,128)S(1)}, f32[12,4096]{1,0:T(8,128)S(1)}, u32[]{:S(2)}, u32[]{:S(2)}) collective-permute-start(f32[12,4096]{1,0:T(8,128)S(1)} %add.811), channel_id=1, source_target_pairs={{0,6},{2,4},{4,2},{6,0},{8,10},{10,8},{12,14},{14,12},{16,22},{18,... | collective-permute-start | bytes 589832 | tf_op jit(solution)/shard_map/ppermute | solution.py:63
  135.2 13.6 %shard_map.93 = bf16[2,800,512]{2,1,0:T(8,128)(2,1)} custom-call(s32[16]{0:T(128)S(1)} %stack.641.idx_ref, bf16[800,8192]{1,0:T(8,128)(2,1)} %bitcast.226, bf16[800,8192]{1,0:T(8,128)(2,1)} %collective-permute-done.10.refs_1_.refs_3_.refs_5_.refs_7_, bf16[800,8192]{1,0:T(8,128)(2,1)} %bitcast.227, ...), custom_call_target="tpu_custom_call" | custom-call | flops 6710886400 | bytes 13107200 | tf_op jit(solution)/shard_map/pallas_call | solution.py:148
  151.6 9.6 %all_to_all.15 = bf16[8,2,64,128]{3,2,1,0:T(8,128)(2,1)S(1)} all-to-all(bf16[8,2,64,128]{3,2,1,0:T(8,128)(2,1)S(1)} %copy.61), channel_id=1, replica_groups=mesh['yh'=2,'z'=4,'c'=2,'x'=4,'yl'=2] {'x','yl'}, dimensions={0} | all-to-all | bytes 524288 | tf_op jit(solution)/shard_map/all_to_all | solution.py:406
  163.6 4.7 %all-to-all-start.1 = ((bf16[8,2,48,128]{3,2,1,0:T(8,128)(2,1)}), bf16[8,2,48,128]{3,2,1,0:T(8,128)(2,1)S(1)}, u32[]{:S(2)}, u32[]{:S(2)}) async-start(bf16[8,2,48,128]{3,2,1,0:T(8,128)(2,1)} %broadcast_in_dim.86), calls=%async_computation.1 | async-start | bytes 393216 | tf_op jit(solution)/shard_map/all_to_all | solution.py:415
  168.4 8.3 %all-to-all-done.1 = bf16[8,2,48,128]{3,2,1,0:T(8,128)(2,1)S(1)} async-done(((bf16[8,2,48,128]{3,2,1,0:T(8,128)(2,1)}), bf16[8,2,48,128]{3,2,1,0:T(8,128)(2,1)S(1)}, u32[]{:S(2)}, u32[]{:S(2)}) %all-to-all-start.1) | async-done | bytes 196640 | tf_op jit(solution)/shard_map/all_to_all | solution.py:415
  178.1 9.2 %all_to_all.16 = f32[8,4,3,512]{3,1,2,0:T(4,128)S(1)} all-to-all(f32[8,4,3,512]{3,1,2,0:T(4,128)S(1)} %copy_select_fusion), channel_id=1, replica_groups=mesh['yh'=2,'z'=4,'c'=2,'x'=4,'yl'=2] {'x','yl'}, dimensions={0} | all-to-all | bytes 393216 | tf_op jit(solution)/shard_map/all_to_all | solution.py:419
  (167 shorter events, 33.6 us)
Async XLA Ops:
  1.7 4.3 %collective-permute-start = (bf16[1024,512]{1,0:T(8,128)(2,1)S(1)}, bf16[1024,512]{1,0:T(8,128)(2,1)}, u32[]{:S(2)}, u32[]{:S(2)}) collective-permute-start(bf16[1024,512]{1,0:T(8,128)(2,1)S(1)} %pad_maximum_fusion.2), channel_id=1, source_target_pairs={{0,8},{2,10},{4,12},{6,14},{8,0},{10,2},{12,4},{14,6},{16,24},{18,... | collective-permute-start | bytes 3145736 | tf_op jit(solution)/shard_map/ppermute | solution.py:63
  8.2 19.2 %copy-start.7 = (bf16[512,256]{1,0:T(8,128)(2,1)}, bf16[512,256]{1,0:T(8,128)(2,1)S(1)}, u32[]{:S(2)}) copy-start(bf16[512,256]{1,0:T(8,128)(2,1)S(1)} %get-tuple-element.64) | copy-start | bytes 786436
  10.7 38.7 %collective-permute-start.10 = (bf16[800,8192]{1,0:T(8,128)(2,1)}, bf16[800,8192]{1,0:T(8,128)(2,1)}, u32[]{:S(2)}, u32[]{:S(2)}) collective-permute-start(bf16[800,8192]{1,0:T(8,128)(2,1)} %bitcast.219), channel_id=1, source_target_pairs={{0,8},{2,10},{4,12},{6,14},{8,0},{10,2},{12,4},{14,6},{16,24},{18,... | collective-permute-start | bytes 39321608 | tf_op jit(solution)/shard_map/ppermute | solution.py:63
  11.2 29.1 %collective-permute-start.1 = (f32[96,4096]{1,0:T(8,128)}, f32[96,4096]{1,0:T(8,128)}, u32[]{:S(2)}, u32[]{:S(2)}) collective-permute-start(f32[96,4096]{1,0:T(8,128)} %fusion.20), channel_id=1, source_target_pairs={{0,8},{2,10},{4,12},{6,14},{8,0},{10,2},{12,4},{14,6},{16,24},{18,... | collective-permute-start | bytes 4718600 | tf_op jit(solution)/shard_map/ppermute | solution.py:63
  11.3 6.4 %collective-permute-start.3 = (bf16[512,256]{1,0:T(8,128)(2,1)S(1)}, bf16[512,256]{1,0:T(8,128)(2,1)S(1)}, u32[]{:S(2)}, u32[]{:S(2)}) collective-permute-start(bf16[512,256]{1,0:T(8,128)(2,1)S(1)} %get-tuple-element.64), channel_id=1, source_target_pairs={{0,16},{2,18},{4,20},{6,22},{8,56},{10,58},{12,60},{14,62},{16,0},... | collective-permute-start | bytes 786440 | tf_op jit(solution)/shard_map/ppermute | solution.py:63
  13.3 12.5 %collective-permute-start.2 = (bf16[256,512]{1,0:T(8,128)(2,1)}, bf16[256,512]{1,0:T(8,128)(2,1)S(1)}, u32[]{:S(2)}, u32[]{:S(2)}) collective-permute-start(bf16[256,512]{1,0:T(8,128)(2,1)} %dynamic-slice_select_fusion), channel_id=1, source_target_pairs={{0,65},{2,67},{4,69},{6,71},{8,73},{10,75},{12,77},{14,79},{16,81}... | collective-permute-start | bytes 786440 | tf_op jit(solution)/shard_map/ppermute | solution.py:63
  18.5 13.1 %collective-permute-start.5 = (bf16[1024,256]{1,0:T(8,128)(2,1)}, bf16[1024,256]{1,0:T(8,128)(2,1)}, u32[]{:S(2)}, u32[]{:S(2)}) collective-permute-start(bf16[1024,256]{1,0:T(8,128)(2,1)} %pad_maximum_fusion.7), channel_id=1, source_target_pairs={{0,48},{2,50},{4,52},{6,54},{8,24},{10,26},{12,28},{14,30},{16,32}... | collective-permute-start | bytes 1572872 | tf_op jit(solution)/shard_map/ppermute | solution.py:63
  22.7 31.5 %collective-permute-start.8 = (bf16[1024,256]{1,0:T(8,128)(2,1)}, bf16[1024,256]{1,0:T(8,128)(2,1)}, u32[]{:S(2)}, u32[]{:S(2)}) collective-permute-start(bf16[1024,256]{1,0:T(8,128)(2,1)} %pad_maximum_fusion.6), channel_id=1, source_target_pairs={{0,65},{2,67},{4,69},{6,71},{8,73},{10,75},{12,77},{14,79},{16,81}... | collective-permute-start | bytes 1572872 | tf_op jit(solution)/shard_map/ppermute | solution.py:63
  26.9 9.3 %collective-permute-start.4 = (bf16[512,512]{1,0:T(8,128)(2,1)S(1)}, bf16[512,512]{1,0:T(8,128)(2,1)S(1)}, u32[]{:S(2)}, u32[]{:S(2)}) collective-permute-start(bf16[512,512]{1,0:T(8,128)(2,1)S(1)} %pad_maximum_fusion.8), channel_id=1, source_target_pairs={{0,16},{2,18},{4,20},{6,22},{8,56},{10,58},{12,60},{14,62},{16,0},... | collective-permute-start | bytes 1572872 | tf_op jit(solution)/shard_map/ppermute | solution.py:63
  27.4 10.4 %copy-start.12 = (bf16[256,512]{1,0:T(8,128)(2,1)S(1)}, bf16[256,512]{1,0:T(8,128)(2,1)}, u32[]{:S(2)}) copy-start(bf16[256,512]{1,0:T(8,128)(2,1)} %copy-done.11) | copy-start | bytes 786436
  36.2 12.2 %collective-permute-start.9 = (bf16[768,512]{1,0:T(8,128)(2,1)S(1)}, bf16[768,512]{1,0:T(8,128)(2,1)}, u32[]{:S(2)}, u32[]{:S(2)}) collective-permute-start(bf16[768,512]{1,0:T(8,128)(2,1)S(1)} %get-tuple-element.67.refs_12_), channel_id=1, source_target_pairs={{0,2},{2,0},{4,6},{6,4},{8,14},{10,12},{12,10},{14,8},{16,18},{18,... | collective-permute-start | bytes 2359304 | tf_op jit(solution)/shard_map/ppermute | solution.py:63
  38.9 25.2 %collective-permute-start.7 = (bf16[1024,512]{1,0:T(8,128)(2,1)}, bf16[1024,512]{1,0:T(8,128)(2,1)S(1)}, u32[]{:S(2)}, u32[]{:S(2)}) collective-permute-start(bf16[1024,512]{1,0:T(8,128)(2,1)} %pad_maximum_fusion.4), channel_id=1, source_target_pairs={{0,48},{2,50},{4,52},{6,54},{8,24},{10,26},{12,28},{14,30},{16,32}... | collective-permute-start | bytes 3145736 | tf_op jit(solution)/shard_map/ppermute | solution.py:63
  42.4 22.5 %collective-permute-start.6 = (f32[48,4096]{1,0:T(8,128)}, f32[48,4096]{1,0:T(8,128)}, u32[]{:S(2)}, u32[]{:S(2)}) collective-permute-start(f32[48,4096]{1,0:T(8,128)} %slice_add_fusion), channel_id=1, source_target_pairs={{0,16},{2,18},{4,20},{6,22},{8,56},{10,58},{12,60},{14,62},{16,0},... | collective-permute-start | bytes 2359304 | tf_op jit(solution)/shard_map/ppermute | solution.py:63
  42.7 22.3 %copy-start.4 = (f32[96,4096]{1,0:T(8,128)S(1)}, f32[96,4096]{1,0:T(8,128)}, u32[]{:S(2)}) copy-start(f32[96,4096]{1,0:T(8,128)} %copy-done.3) | copy-start | bytes 4718596
  48.4 18.1 %collective-permute-start.12 = (bf16[2048,256]{1,0:T(8,128)(2,1)}, bf16[2048,256]{1,0:T(8,128)(2,1)S(1)}, u32[]{:S(2)}, u32[]{:S(2)}) collective-permute-start(bf16[2048,256]{1,0:T(8,128)(2,1)} %pad_maximum_fusion.3), channel_id=1, source_target_pairs={{0,1},{2,3},{4,5},{6,7},{8,73},{10,75},{12,77},{14,79},{16,17},{18... | collective-permute-start | bytes 3145736 | tf_op jit(solution)/shard_map/ppermute | solution.py:63
  51.5 35.0 %collective-permute-start.16 = (bf16[1536,512]{1,0:T(8,128)(2,1)}, bf16[1536,512]{1,0:T(8,128)(2,1)S(1)}, u32[]{:S(2)}, u32[]{:S(2)}) collective-permute-start(bf16[1536,512]{1,0:T(8,128)(2,1)} %constant_dynamic-update-slice_fusion.2), channel_id=1, source_target_pairs={{0,6},{2,4},{4,2},{6,0},{8,10},{10,8},{12,14},{14,12},{16,22},{18,... | collective-permute-start | bytes 4718600 | tf_op jit(solution)/shard_map/ppermute | solution.py:63
  55.4 14.0 %copy-start.8 = (bf16[512,256]{1,0:T(8,128)(2,1)S(1)}, bf16[512,256]{1,0:T(8,128)(2,1)}, u32[]{:S(2)}) copy-start(bf16[512,256]{1,0:T(8,128)(2,1)} %copy-done.7) | copy-start | bytes 786436
  55.4 14.0 %copy-start.10 = (bf16[512,256]{1,0:T(8,128)(2,1)S(1)}, bf16[512,256]{1,0:T(8,128)(2,1)}, u32[]{:S(2)}) copy-start(bf16[512,256]{1,0:T(8,128)(2,1)} %copy-done.9) | copy-start | bytes 786436
  55.4 24.6 %collective-permute-start.14 = (bf16[2048,256]{1,0:T(8,128)(2,1)S(1)}, bf16[2048,256]{1,0:T(8,128)(2,1)S(1)}, u32[]{:S(2)}, u32[]{:S(2)}) collective-permute-start(bf16[2048,256]{1,0:T(8,128)(2,1)S(1)} %pad_maximum_fusion.5), channel_id=1, source_target_pairs={{0,16},{2,18},{4,20},{6,22},{8,56},{10,58},{12,60},{14,62},{16,0},... | collective-permute-start | bytes 3145736 | tf_op jit(solution)/shard_map/ppermute | solution.py:63
  64.1 36.6 %collective-permute-start.19 = (bf16[1024,512]{1,0:T(8,128)(2,1)S(1)}, bf16[1024,512]{1,0:T(8,128)(2,1)S(1)}, u32[]{:S(2)}, u32[]{:S(2)}) collective-permute-start(bf16[1024,512]{1,0:T(8,128)(2,1)S(1)} %collective-permute-done.7.refs_8_), channel_id=1, source_target_pairs={{0,2},{2,0},{4,6},{6,4},{8,14},{10,12},{12,10},{14,8},{16,18},{18,... | collective-permute-start | bytes 3145736 | tf_op jit(solution)/shard_map/ppermute | solution.py:63
  66.5 10.4 %collective-permute-start.11 = (f32[24,4096]{1,0:T(8,128)S(1)}, f32[24,4096]{1,0:T(8,128)S(1)}, u32[]{:S(2)}, u32[]{:S(2)}) collective-permute-start(f32[24,4096]{1,0:T(8,128)S(1)} %slice.82), channel_id=1, source_target_pairs={{0,65},{2,67},{4,69},{6,71},{8,73},{10,75},{12,77},{14,79},{16,81}... | collective-permute-start | bytes 1179656 | tf_op jit(solution)/shard_map/ppermute | solution.py:63
  71.9 34.8 %collective-permute-start.18 = (bf16[4096,256]{1,0:T(8,128)(2,1)}, bf16[4096,256]{1,0:T(8,128)(2,1)}, u32[]{:S(2)}, u32[]{:S(2)}) collective-permute-start(bf16[4096,256]{1,0:T(8,128)(2,1)} %pad_maximum_fusion.refs_4_.refs_8_), channel_id=1, source_target_pairs={{0,65},{2,67},{4,69},{6,71},{8,9},{10,11},{12,13},{14,15},{16,81},... | collective-permute-start | bytes 6291464 | tf_op jit(solution)/shard_map/ppermute | solution.py:63
  77.0 7.7 %collective-permute-start.13 = (f32[12,4096]{1,0:T(8,128)S(1)}, f32[12,4096]{1,0:T(8,128)S(1)}, u32[]{:S(2)}, u32[]{:S(2)}) collective-permute-start(f32[12,4096]{1,0:T(8,128)S(1)} %slice.84), channel_id=1, source_target_pairs={{0,48},{2,50},{4,52},{6,54},{8,24},{10,26},{12,28},{14,30},{16,32}... | collective-permute-start | bytes 589832 | tf_op jit(solution)/shard_map/ppermute | solution.py:63
  82.5 27.6 %collective-permute-start.20 = (bf16[4096,256]{1,0:T(8,128)(2,1)}, bf16[4096,256]{1,0:T(8,128)(2,1)}, u32[]{:S(2)}, u32[]{:S(2)}) collective-permute-start(bf16[4096,256]{1,0:T(8,128)(2,1)} %pad_maximum_fusion.1.refs_6_.refs_10_), channel_id=1, source_target_pairs={{0,48},{2,50},{4,52},{6,54},{8,24},{10,26},{12,28},{14,30},{16,32}... | collective-permute-start | bytes 6291464 | tf_op jit(solution)/shard_map/ppermute | solution.py:63
  84.7 16.0 %collective-permute-start.15 = (f32[12,4096]{1,0:T(8,128)S(1)}, f32[12,4096]{1,0:T(8,128)S(1)}, u32[]{:S(2)}, u32[]{:S(2)}) collective-permute-start(f32[12,4096]{1,0:T(8,128)S(1)} %slice_add_fusion.3), channel_id=1, source_target_pairs={{0,1},{2,3},{4,5},{6,7},{8,9},{10,11},{12,13},{14,15},{16,17},{18,... | collective-permute-start | bytes 589832 | tf_op jit(solution)/shard_map/ppermute | solution.py:63
  102.8 32.4 %collective-permute-start.22 = (bf16[2048,512]{1,0:T(8,128)(2,1)}, bf16[2048,512]{1,0:T(8,128)(2,1)}, u32[]{:S(2)}, u32[]{:S(2)}) collective-permute-start(bf16[2048,512]{1,0:T(8,128)(2,1)} %constant_dynamic-update-slice_fusion.5), channel_id=1, source_target_pairs={{0,6},{2,4},{4,2},{6,0},{8,10},{10,8},{12,14},{14,12},{16,22},{18,... | collective-permute-start | bytes 6291464 | tf_op jit(solution)/shard_map/ppermute | solution.py:63
  106.5 25.2 %collective-permute-start.17 = (f32[12,4096]{1,0:T(8,128)S(1)}, f32[12,4096]{1,0:T(8,128)S(1)}, u32[]{:S(2)}, u32[]{:S(2)}) collective-permute-start(f32[12,4096]{1,0:T(8,128)S(1)} %add.755), channel_id=1, source_target_pairs={{0,2},{2,0},{4,6},{6,4},{8,14},{10,12},{12,10},{14,8},{16,18},{18,... | collective-permute-start | bytes 589832 | tf_op jit(solution)/shard_map/ppermute | solution.py:63
  131.7 17.2 %collective-permute-start.21 = (f32[12,4096]{1,0:T(8,128)S(1)}, f32[12,4096]{1,0:T(8,128)S(1)}, u32[]{:S(2)}, u32[]{:S(2)}) collective-permute-start(f32[12,4096]{1,0:T(8,128)S(1)} %add.811), channel_id=1, source_target_pairs={{0,6},{2,4},{4,2},{6,0},{8,10},{10,8},{12,14},{14,12},{16,22},{18,... | collective-permute-start | bytes 589832 | tf_op jit(solution)/shard_map/ppermute | solution.py:63
  151.5 25.3 %copy-start.15 = (bf16[1024,512]{1,0:T(8,128)(2,1)S(1)}, bf16[1024,512]{1,0:T(8,128)(2,1)}, u32[]{:S(2)}) copy-start(bf16[1024,512]{1,0:T(8,128)(2,1)} %param.17) | copy-start | bytes 3145732
  161.6 1.3 collective-permute-start.23
  162.9 25.0 %copy-start.1 = (bf16[64,8192]{1,0:T(8,128)(2,1)S(1)}, bf16[64,8192]{1,0:T(8,128)(2,1)}, u32[]{:S(2)}) copy-start(bf16[64,8192]{1,0:T(8,128)(2,1)} %param.13) | copy-start | bytes 3145732
  163.6 13.1 %all-to-all-start.1 = ((bf16[8,2,48,128]{3,2,1,0:T(8,128)(2,1)}), bf16[8,2,48,128]{3,2,1,0:T(8,128)(2,1)S(1)}, u32[]{:S(2)}, u32[]{:S(2)}) async-start(bf16[8,2,48,128]{3,2,1,0:T(8,128)(2,1)} %broadcast_in_dim.86), calls=%async_computation.1 | async-start | bytes 393216 | tf_op jit(solution)/shard_map/all_to_all | solution.py:415
  (15 other events, 63.9 us)
